TPU v7x, 256 devices: a whole 4x4x8 slice. The times are simulated.
256 devices in a mesh: px: 8 (over z_lo, core), py: 32 (over z_hi, x, y).
Axes of the slice: x: 4, y: 4, z: 8 (z_hi: 2, z_lo: 4; z = z_hi * 4 + z_lo), core: 2. Of those that a mesh axis runs over, the one named last changes fastest.
Arguments:
- charges: float32 [8, 32, 512], P('px', 'py'), may hold values from -4 to 4
- cells: int32 [3, 8, 32, 512], P(None, 'px', 'py'), may hold values from 0 to 383, as said below
- fractions: float32 [3, 8, 32, 512], P(None, 'px', 'py'), may hold values from 0 to 1
- filled: int32 [8, 32], P('px', 'py'), may hold values from 256 to 512, as said below
Outputs:
- potentials: float32 [8, 32, 512], P('px', 'py')
- forces: float32 [3, 8, 32, 512], P(None, 'px', 'py')
Inputs may be any that keep to these rules, and one draw needn't show every extreme that they name: `cells`: component 0 lies in 0 .. 47, component 1 in 0 .. 11, component 2 in 0 .. 383. Slots at or beyond filled are padding; some brick is full in every draw.
All inputs are finite; a program needn't handle non-finite values.
Results may differ from a plain program's by a relative error of at most 0.0003.
Values sent between devices are 32-bit elements; how exact they have to be, the bound alone decides.
A program may use at most 128 MiB of HBM per device.

v0:
```python
import math

import jax
import jax.numpy as jnp
from jax import lax
from jax.sharding import PartitionSpec as P

GRID = 384
ORDER = 6


SPLITTING = 1.6
COUPLING = 1.0 / math.pi
PRECISE = lax.Precision.HIGHEST


def from_behind(value, axis, steps):
    count = lax.axis_size(axis)
    pairs = [(source, (source + steps) % count) for source in range(count)]
    return lax.ppermute(value, axis, pairs)


def spline_tables(fraction):
    values = [1.0 - fraction, fraction]
    previous = values
    for k in range(2, ORDER):
        previous = values
        zeroed = jnp.zeros_like(fraction)
        updated = []
        for j in range(k + 1):
            preceding = values[j - 1] if j >= 1 else zeroed
            current = values[j] if j < k else zeroed
            updated.append(((fraction + (k - j)) * preceding + (1.0 - fraction + j) * current) / k)
        values = updated
    zeroed = jnp.zeros_like(fraction)
    slopes = []
    for j in range(ORDER):
        preceding = previous[j - 1] if j >= 1 else zeroed
        current = previous[j] if j < ORDER - 1 else zeroed
        slopes.append(preceding - current)
    return (jnp.stack(values), jnp.stack(slopes))


def stencil_tables(starts, values, slopes, length, period):
    places = lax.broadcasted_iota(jnp.int32, (length, starts.shape[0]), 0)
    weight_table = jnp.zeros((length, starts.shape[0]), jnp.float32)
    slope_table = jnp.zeros((length, starts.shape[0]), jnp.float32)
    for j in range(ORDER):
        target = starts + j
        if period > 0:
            target = target % period
        matches = places == target[None, :]
        weight_table = weight_table + jnp.where(matches, values[j][None, :], 0.0)
        slope_table = slope_table + jnp.where(matches, slopes[j][None, :], 0.0)
    return (weight_table, slope_table)


def brick_tables(cell_rows, fraction_rows, wide_x, wide_y):
    values, slopes = spline_tables(fraction_rows)
    margin = ORDER - 1
    table_x = stencil_tables(cell_rows[0], values[:, 0], slopes[:, 0], wide_x + margin, 0)
    table_y = stencil_tables(cell_rows[1], values[:, 1], slopes[:, 1], wide_y + margin, 0)
    table_z = stencil_tables(cell_rows[2], values[:, 2], slopes[:, 2], GRID, GRID)
    return table_x + table_y + table_z


def spread_brick(weighted, tables):
    weight_x, slope_x, weight_y, slope_y, weight_z, slope_z = tables
    columns = (weight_x * weighted[None, :])[:, None, :] * weight_y[None, :, :]
    flattened = columns.reshape(-1, columns.shape[2])
    cell_grid = lax.dot_general(
        flattened,
        weight_z,
        (((1,), (1,)), ((), ())),
        precision=PRECISE,
        preferred_element_type=jnp.float32,
    )
    return cell_grid.reshape(weight_x.shape[0], weight_y.shape[0], weight_z.shape[0])


def sample_brick(grid_ext, tables, weighted):
    weight_x, slope_x, weight_y, slope_y, weight_z, slope_z = tables
    size_x = weight_x.shape[0]
    size_y = weight_y.shape[0]
    number = weight_z.shape[1]
    flattened = grid_ext.reshape(size_x * size_y, grid_ext.shape[2])
    paired = jnp.concatenate([weight_z, slope_z], axis=1)
    sampled = jnp.dot(flattened, paired, precision=PRECISE, preferred_element_type=jnp.float32)
    level = sampled[:, :number].reshape(size_x, size_y, number)
    rising = sampled[:, number:].reshape(size_x, size_y, number)
    over_y = jnp.sum(weight_y[None] * level, axis=1)
    slope_over_y = jnp.sum(slope_y[None] * level, axis=1)
    rising_over_y = jnp.sum(weight_y[None] * rising, axis=1)
    potential = jnp.sum(weight_x * over_y, axis=0)
    gradient = jnp.stack(
        [
            jnp.sum(slope_x * over_y, axis=0),
            jnp.sum(weight_x * slope_over_y, axis=0),
            jnp.sum(weight_x * rising_over_y, axis=0),
        ]
    )
    return (potential, -weighted[None, :] * gradient)


def axis_terms(indices):
    signed = jnp.where(indices <= GRID // 2, indices, indices - GRID).astype(jnp.float32) / GRID
    values, slopes = spline_tables(jnp.zeros((1,), jnp.float32))
    cosine_sum = jnp.zeros(indices.shape, jnp.float32)
    sine_sum = jnp.zeros(indices.shape, jnp.float32)
    for j in range(ORDER - 1):
        angles = 2.0 * math.pi / GRID * (indices * j % GRID).astype(jnp.float32)
        cosine_sum = cosine_sum + values[j, 0] * jnp.cos(angles)
        sine_sum = sine_sum + values[j, 0] * jnp.sin(angles)
    return (signed * signed, 1.0 / (cosine_sum * cosine_sum + sine_sum * sine_sum))


def green(freq_x, freq_y, freq_z):
    square_x, modulus_x = axis_terms(freq_x)
    square_y, modulus_y = axis_terms(freq_y)
    square_z, modulus_z = axis_terms(freq_z)
    squared = square_x + square_y + square_z
    positive = squared > 0.0
    bounded = jnp.where(positive, squared, 1.0)
    factor = COUPLING / float(GRID * GRID * GRID)
    damping = jnp.exp(-(math.pi * math.pi / (SPLITTING * SPLITTING)) * bounded)
    return jnp.where(positive, factor * damping / bounded * modulus_x * modulus_y * modulus_z, 0.0)


def dft_tables(inputs_at, outputs_at):
    products = inputs_at[:, None] * outputs_at[None, :] % GRID
    angles = 2.0 * math.pi / GRID * products.astype(jnp.float32)
    return (jnp.cos(angles), jnp.sin(angles))


def positions():
    return jnp.arange(GRID, dtype=jnp.int32)


def transform(layers, pattern, inputs_at, outputs_at, inverse, real_out):
    cosines, sines = dft_tables(inputs_at, outputs_at)

    def multiply(operand, table):
        return jnp.einsum(
            pattern, operand, table, precision=PRECISE, preferred_element_type=jnp.float32
        )

    if layers.shape[0] == 1:
        return jnp.stack([multiply(layers[0], cosines), -multiply(layers[0], sines)])
    direction = 1.0 if inverse else -1.0
    real_part = multiply(layers[0], cosines) - direction * multiply(layers[1], sines)
    if real_out:
        return real_part[None]
    imag_part = multiply(layers[1], cosines) + direction * multiply(layers[0], sines)
    return jnp.stack([real_part, imag_part])


def columns_py(layers):
    return lax.all_to_all(layers, "py", split_axis=2, concat_axis=3, tiled=True)


def columns_px(layers):
    return lax.all_to_all(layers, "px", split_axis=2, concat_axis=3, tiled=True)


def neighbour_px(rim_rows, offset):
    return from_behind(rim_rows, "px", offset)


def neighbour_py(rim_rows, offset):
    return from_behind(rim_rows, "py", offset)


def fold_ghosts(cell_grid, wide_x, wide_y, margin):
    incoming = neighbour_px(cell_grid[wide_x:], 1)
    cell_grid = jnp.concatenate([cell_grid[:margin] + incoming, cell_grid[margin:wide_x]], axis=0)
    incoming = neighbour_py(cell_grid[:, wide_y:], 1)
    return jnp.concatenate([cell_grid[:, :margin] + incoming, cell_grid[:, margin:wide_y]], axis=1)


def extend_rims(potential_grid, margin):
    potential_grid = jnp.concatenate(
        [potential_grid, neighbour_px(potential_grid[:margin], -1)], axis=0
    )
    return jnp.concatenate([potential_grid, neighbour_py(potential_grid[:, :margin], -1)], axis=1)


def shards(charges, cells, fractions, filled):
    count_px = lax.axis_size("px")
    count_py = lax.axis_size("py")
    wide_x = GRID // count_px
    wide_y = GRID // count_py
    margin = ORDER - 1
    slot_count = charges.shape[2]
    occupied = (lax.broadcasted_iota(jnp.int32, (slot_count,), 0) < filled[0, 0]).astype(
        jnp.float32
    )
    weighted = charges[0, 0] * occupied
    tables = brick_tables(cells[:, 0, 0, :], fractions[:, 0, 0, :], wide_x, wide_y)
    cell_grid = spread_brick(weighted, tables)
    cell_grid = fold_ghosts(cell_grid, wide_x, wide_y, margin)
    ordinal = jnp.arange(GRID, dtype=jnp.int32)
    place_x = positions()
    place_y = positions()
    layers = transform(cell_grid[None], "xyz,zk->xky", ordinal, ordinal, False, False)
    layers = columns_py(layers)
    layers = transform(layers, "xzy,yk->zkx", place_y, ordinal, False, False)
    layers = columns_px(layers)
    layers = transform(layers, "zyx,xk->zyk", place_x, ordinal, False, False)
    depth_z = layers.shape[1]
    depth_y = layers.shape[2]
    freq_z = lax.axis_index("py") * depth_z + jnp.arange(depth_z, dtype=jnp.int32)
    freq_y = lax.axis_index("px") * depth_y + jnp.arange(depth_y, dtype=jnp.int32)
    multiplier = green(ordinal[None, None, :], freq_y[None, :, None], freq_z[:, None, None])
    layers = layers * multiplier[None]
    layers = transform(layers, "zyk,kx->zxy", ordinal, place_x, True, False)
    layers = columns_px(layers)
    layers = transform(layers, "zxy,yk->xkz", ordinal, place_y, True, False)
    layers = columns_py(layers)
    potential_grid = transform(layers, "xyz,zk->xyk", ordinal, ordinal, True, True)[0]
    potential_grid = extend_rims(potential_grid, margin)
    potentials, forces = sample_brick(potential_grid, tables, weighted)
    return ((potentials * occupied).reshape(1, 1, slot_count), forces.reshape(3, 1, 1, slot_count))


def solution(mesh):
    placed = (
        P("px", "py", None),
        P(None, "px", "py", None),
        P(None, "px", "py", None),
        P("px", "py"),
    )
    return jax.shard_map(
        shards,
        mesh=mesh,
        in_specs=placed,
        out_specs=(P("px", "py", None), P(None, "px", "py", None)),
        check_vma=False,
    )
```

profile of v0, /device:TPU:1, one launch (start us, length us, event | category | flops | bytes accessed | tf_op | source)
XLA Modules:
  0.0 569.2 jit_solution(10543048712554544429)
XLA Ops:
  14.3 5.1 fusion.275
  27.0 15.8 %collective-permute-done.1 = f32[48,5,384]{2,0,1:T(8,128)S(1)} collective-permute-done((f32[48,5,384]{2,0,1:T(8,128)S(1)}, f32[48,5,384]{2,0,1:T(8,128)S(1)}, u32[]{:S(2)}, u32[]{:S(2)}) %collective-permute-start.1) | collective-permute-done | bytes 368672 | tf_op jit(solution)/shard_map/ppermute | solution.py:20
  42.9 4.1 convolution_bitcast_fusion
  51.2 5.6 copy.62
  56.8 10.0 %reshape.2050 = f32[32,1,13824]{2,1,0:T(1,128)S(1)} reshape(f32[384,12,2,48]{3,2,1,0:T(2,128)} %bitcast.326) | data formatting | bytes 3538944
  66.8 24.9 %all_to_all.60 = f32[32,1,13824]{2,1,0:T(1,128)S(1)} all-to-all(f32[32,1,13824]{2,1,0:T(1,128)S(1)} %reshape.2050), channel_id=1, replica_groups=mesh['px'=8,'py'=32] {'py'}, dimensions={0} | all-to-all | bytes 3538944 | tf_op jit(solution)/shard_map/all_to_all | solution.py:158
  92.3 4.8 reduce
  97.1 9.4 %reshape.2051 = f32[384,12,2,48]{3,2,1,0:T(2,128)} reshape(f32[32,13824]{1,0:T(8,128)S(1)} %reduce) | data formatting | bytes 3538944
  106.5 10.0 %fusion.287 = (f32[1,48,12,32,12]{1,0,4,2,3:T(1,128)S(1)}, f32[1,48,12,32,12]{1,0,4,2,3:T(1,128)}) fusion(f32[2,48,12,32,12]{1,0,4,2,3:T(2,128)} %bitcast.322), kind=kLoop, calls=%fused_computation.384 | loop fusion | bytes 3538944 | tf_op jit(solution)/shard_map/slice | solution.py:150
  121.0 6.0 %fusion.50 = f32[384,48,12]{0,1,2:T(8,128)S(1)} fusion(f32[48,12,384]{0,2,1:T(8,128)S(1)} %squeeze.29), kind=kOutput, calls=%fused_computation.90 | convolution fusion | flops 1020542976 | bytes 1769472 | tf_op jit(solution)/shard_map/xzy,yk->zkx/dot_general | solution.py:143
  128.9 4.1 squeeze.30
  133.1 7.8 %fusion.48 = f32[384,48,12]{0,1,2:T(8,128)S(1)} fusion(f32[48,12,384]{0,2,1:T(8,128)} %squeeze.30), kind=kOutput, calls=%fused_computation.88 | convolution fusion | flops 1020542976 | bytes 1769472 | tf_op jit(solution)/shard_map/xzy,yk->zkx/dot_general | solution.py:143
  140.9 6.1 %fusion.13 = f32[1,12,384,48]{2,3,1,0:T(8,128)S(1)} fusion(f32[384,48,12]{0,1,2:T(8,128)S(1)} %fusion.50, f32[48,12,384]{0,2,1:T(8,128)S(1)} %copy-done), kind=kOutput, calls=%fused_computation.35 | convolution fusion | flops 1020985344 | bytes 2654208 | tf_op jit(solution)/shard_map/xzy,yk->zkx/dot_general | solution.py:143
  147.0 6.4 %fusion.11 = f32[1,12,384,48]{2,3,1,0:T(8,128)S(1)} fusion(f32[384,48,12]{0,1,2:T(8,128)S(1)} %fusion.48, f32[48,12,384]{0,2,1:T(8,128)S(1)} %squeeze.29), kind=kOutput, calls=%fused_computation.32 | convolution fusion | flops 1020985344 | bytes 2654208 | tf_op jit(solution)/shard_map/xzy,yk->zkx/dot_general | solution.py:143
  153.5 5.3 copy.69
  158.9 10.2 %reshape.2052 = f32[8,1,55296]{2,1,0:T(1,128)} reshape(f32[384,12,2,48]{3,2,1,0:T(2,128)} %bitcast.327) | data formatting | bytes 3538944
  169.1 39.2 %all-to-all-start.1 = ((f32[8,1,55296]{2,1,0:T(1,128)}), f32[8,1,55296]{2,1,0:T(1,128)S(1)}, u32[]{:S(2)}, u32[]{:S(2)}) async-start(f32[8,1,55296]{2,1,0:T(1,128)} %reshape.2052), calls=%async_computation.1 | async-start | bytes 3538944 | tf_op jit(solution)/shard_map/all_to_all | solution.py:162
  210.1 39.3 %all-to-all-done.1 = f32[8,1,55296]{2,1,0:T(1,128)S(1)} async-done(((f32[8,1,55296]{2,1,0:T(1,128)}), f32[8,1,55296]{2,1,0:T(1,128)S(1)}, u32[]{:S(2)}, u32[]{:S(2)}) %all-to-all-start.1) | async-done | bytes 1769504 | tf_op jit(solution)/shard_map/all_to_all | solution.py:162
  249.4 4.8 reduce.1
  254.3 9.8 %reshape.2053 = f32[384,12,2,48]{3,2,1,0:T(2,128)} reshape(f32[8,55296]{1,0:T(8,128)S(1)} %reduce.1) | data formatting | bytes 3538944
  264.1 5.2 copy.89
  273.3 5.0 convolution_multiply_fusion.1
  279.9 5.3 convolution_multiply_fusion
  285.3 4.5 fusion.9
  298.1 4.3 fusion.25
  302.4 4.1 fusion.7
  306.5 4.1 fusion.6
  310.8 5.3 copy.71
  316.1 9.2 %reshape.2054 = f32[8,1,55296]{2,1,0:T(1,128)S(1)} reshape(f32[384,12,2,48]{3,2,1,0:T(2,128)} %bitcast.329) | data formatting | bytes 3538944
  325.3 44.4 %all_to_all.61 = f32[8,1,55296]{2,1,0:T(1,128)S(1)} all-to-all(f32[8,1,55296]{2,1,0:T(1,128)S(1)} %reshape.2054), channel_id=1, replica_groups=mesh['px'=8,'py'=32] {'px'}, dimensions={0} | all-to-all | bytes 3538944 | tf_op jit(solution)/shard_map/all_to_all | solution.py:162
  369.7 4.8 reduce.2
  374.6 9.8 %reshape.2055 = f32[384,12,2,48]{3,2,1,0:T(2,128)} reshape(f32[8,55296]{1,0:T(8,128)S(1)} %reduce.2) | data formatting | bytes 3538944
  384.4 5.1 copy.88
  393.6 5.0 fusion.42
  400.2 5.3 fusion.40
  405.5 4.5 fusion.5
  410.1 4.1 fusion.4
  414.3 5.3 copy.73
  419.7 10.0 %reshape.2056 = f32[32,1,13824]{2,1,0:T(1,128)S(1)} reshape(f32[384,12,2,48]{3,2,1,0:T(2,128)} %bitcast.331) | data formatting | bytes 3538944
  429.7 46.9 %all_to_all.62 = f32[32,1,13824]{2,1,0:T(1,128)S(1)} all-to-all(f32[32,1,13824]{2,1,0:T(1,128)S(1)} %reshape.2056), channel_id=1, replica_groups=mesh['px'=8,'py'=32] {'py'}, dimensions={0} | all-to-all | bytes 3538944 | tf_op jit(solution)/shard_map/all_to_all | solution.py:158
  476.6 4.8 reduce.3
  481.4 9.1 %reshape.2057 = f32[384,12,2,48]{3,2,1,0:T(2,128)} reshape(f32[32,13824]{1,0:T(8,128)S(1)} %reduce.3) | data formatting | bytes 3538944
  490.6 10.0 %fusion.284 = (f32[1,48,12,32,12]{1,0,4,2,3:T(1,128)}, f32[1,48,12,32,12]{1,0,4,2,3:T(1,128)S(1)}) fusion(f32[2,48,12,32,12]{1,0,4,2,3:T(2,128)} %bitcast.325), kind=kLoop, calls=%fused_computation.381 | loop fusion | bytes 3538944 | tf_op jit(solution)/shard_map/slice | solution.py:150
  502.4 8.8 %fusion.38 = f32[48,12,384]{2,0,1:T(8,128)} fusion(f32[48,12,384]{0,2,1:T(8,128)} %squeeze.68), kind=kOutput, calls=%fused_computation.78 | convolution fusion | flops 1020542976 | bytes 1769472 | tf_op jit(solution)/shard_map/xyz,zk->xyk/dot_general | solution.py:143
  513.4 7.9 %convolution_subtract_fusion.3 = f32[48,12,384]{2,0,1:T(8,128)S(1)} fusion(f32[48,12,384]{2,0,1:T(8,128)} %fusion.38, f32[48,12,384]{0,2,1:T(8,128)} %squeeze.69), kind=kOutput, calls=%fused_computation.29 | convolution fusion | flops 1020764160 | bytes 2654208 | tf_op jit(solution)/shard_map/xyz,zk->xyk/dot_general | solution.py:143
  524.6 9.2 %collective-permute-done.2 = f32[5,12,384]{2,0,1:T(8,128)S(1)} collective-permute-done((f32[5,12,384]{2,0,1:T(8,128)S(1)}, f32[5,12,384]{2,0,1:T(8,128)S(1)}, u32[]{:S(2)}, u32[]{:S(2)}) %collective-permute-start.2) | collective-permute-done | bytes 92192 | tf_op jit(solution)/shard_map/ppermute | solution.py:20
  536.3 12.5 %collective-permute-done.3 = f32[53,5,384]{2,0,1:T(8,128)S(1)} collective-permute-done((f32[53,5,384]{2,0,1:T(8,128)S(1)}, f32[53,5,384]{2,0,1:T(8,128)S(1)}, u32[]{:S(2)}, u32[]{:S(2)}) %collective-permute-start.3) | collective-permute-done | bytes 407072 | tf_op jit(solution)/shard_map/ppermute | solution.py:20
  549.6 7.5 %fusion = f32[901,1024]{1,0:T(8,128)S(1)} fusion(f32[901,384]{1,0:T(8,128)S(1)} %reshape.2045, f32[384,512]{1,0:T(8,128)} %get-tuple-element.40, f32[384,512]{1,0:T(8,128)} %get-tuple-element.39), kind=kOutput, calls=%fused_computation.10 | convolution fusion | flops 4251844608 | bytes 6647296 | tf_op jit(solution)/shard_map/dot_general | solution.py:88
  (209 shorter events, 75.2 us)
Async XLA Ops:
  5.6 5.9 %copy-start.15 = (f32[1,1,512]{2,0,1:T(1,128)}, f32[1,1,512]{2,0,1:T(1,128)S(1)}, u32[]{:S(2)}) copy-start(f32[1,1,512]{2,0,1:T(1,128)S(1)} %get-tuple-element.84) | copy-start | bytes 6148
  5.6 8.5 %copy-start.48 = (f32[1,1,512]{2,0,1:T(1,128)}, f32[1,1,512]{2,0,1:T(1,128)S(1)}, u32[]{:S(2)}) copy-start(f32[1,1,512]{2,0,1:T(1,128)S(1)} %get-tuple-element.82) | copy-start | bytes 6148
  7.0 4.5 copy-start.17
  7.0 4.5 copy-start.19
  7.0 4.5 copy-start.21
  7.0 4.5 copy-start.23
  7.0 4.5 copy-start.25
  7.7 6.5 %copy-start.34 = (f32[1,1,512]{2,0,1:T(1,128)}, f32[1,1,512]{2,0,1:T(1,128)S(1)}, u32[]{:S(2)}) copy-start(f32[1,1,512]{2,0,1:T(1,128)S(1)} %get-tuple-element.85) | copy-start | bytes 6148
  7.7 6.5 %copy-start.36 = (f32[1,1,512]{2,0,1:T(1,128)}, f32[1,1,512]{2,0,1:T(1,128)S(1)}, u32[]{:S(2)}) copy-start(f32[1,1,512]{2,0,1:T(1,128)S(1)} %get-tuple-element.115) | copy-start | bytes 6148
  8.3 5.9 %copy-start.39 = (f32[1,1,512]{2,0,1:T(1,128)}, f32[1,1,512]{2,0,1:T(1,128)S(1)}, u32[]{:S(2)}) copy-start(f32[1,1,512]{2,0,1:T(1,128)S(1)} %get-tuple-element.109) | copy-start | bytes 6148
  8.9 5.3 copy-start.42
  9.5 4.7 copy-start.45
  14.1 5.2 copy-start.51
  14.1 5.3 copy-start.53
  14.1 5.2 copy-start.55
  14.1 5.2 copy-start.57
  14.2 5.2 copy-start.59
  14.2 5.2 copy-start.61
  19.5 5.9 %collective-permute-start = (f32[5,17,384]{2,0,1:T(8,128)S(1)}, f32[5,17,384]{2,0,1:T(8,128)S(1)}, u32[]{:S(2)}, u32[]{:S(2)}) collective-permute-start(f32[5,17,384]{2,0,1:T(8,128)S(1)} %copy.59), channel_id=1, source_target_pairs={{0,32},{32,64},{64,96},{96,128},{128,160},{160,192},{192,224},{224... | collective-permute-start | bytes 391688 | tf_op jit(solution)/shard_map/ppermute | solution.py:20
  25.5 17.3 %collective-permute-start.1 = (f32[48,5,384]{2,0,1:T(8,128)S(1)}, f32[48,5,384]{2,0,1:T(8,128)S(1)}, u32[]{:S(2)}, u32[]{:S(2)}) collective-permute-start(f32[48,5,384]{2,0,1:T(8,128)S(1)} %pad_maximum_fusion.6), channel_id=1, source_target_pairs={{0,1},{1,2},{2,3},{3,4},{4,5},{5,6},{6,7},{7,8},{8,9},{9,10},{10,1... | collective-permute-start | bytes 1105928 | tf_op jit(solution)/shard_map/ppermute | solution.py:20
  121.0 6.0 %copy-start.2 = (f32[1,48,12,32,12]{1,0,4,2,3:T(1,128)S(1)}, f32[1,48,12,32,12]{1,0,4,2,3:T(1,128)}, u32[]{:S(2)}) copy-start(f32[1,48,12,32,12]{1,0,4,2,3:T(1,128)} %get-tuple-element.32) | copy-start | bytes 2654212
  133.0 7.8 %copy-start = (f32[48,12,384]{0,2,1:T(8,128)S(1)}, f32[48,12,384]{0,2,1:T(8,128)}, u32[]{:S(2)}) copy-start(f32[48,12,384]{0,2,1:T(8,128)} %squeeze.30) | copy-start | bytes 2654212
  169.1 80.4 %all-to-all-start.1 = ((f32[8,1,55296]{2,1,0:T(1,128)}), f32[8,1,55296]{2,1,0:T(1,128)S(1)}, u32[]{:S(2)}, u32[]{:S(2)}) async-start(f32[8,1,55296]{2,1,0:T(1,128)} %reshape.2052), calls=%async_computation.1 | async-start | bytes 3538944 | tf_op jit(solution)/shard_map/all_to_all | solution.py:162
  279.9 5.3 copy-start.3
  279.9 5.3 copy-start.6
  400.2 5.3 copy-start.4
  400.2 5.3 copy-start.7
  502.4 8.8 %copy-start.1 = (f32[1,48,12,32,12]{1,0,4,2,3:T(1,128)S(1)}, f32[1,48,12,32,12]{1,0,4,2,3:T(1,128)}, u32[]{:S(2)}) copy-start(f32[1,48,12,32,12]{1,0,4,2,3:T(1,128)} %get-tuple-element.25) | copy-start | bytes 2654212
  513.2 21.0 %copy-start.32 = (f32[1,1,512]{2,0,1:T(1,128)S(1)}, f32[1,1,512]{2,0,1:T(1,128)}, u32[]{:S(2)}) copy-start(f32[1,1,512]{2,0,1:T(1,128)} %get-tuple-element.61) | copy-start | bytes 6148
  513.2 21.0 %copy-start.33 = (f32[1,1,512]{2,0,1:T(1,128)S(1)}, f32[1,1,512]{2,0,1:T(1,128)}, u32[]{:S(2)}) copy-start(f32[1,1,512]{2,0,1:T(1,128)} %get-tuple-element.111) | copy-start | bytes 6148
  513.2 21.0 %copy-start.35 = (f32[1,1,512]{2,0,1:T(1,128)S(1)}, f32[1,1,512]{2,0,1:T(1,128)}, u32[]{:S(2)}) copy-start(f32[1,1,512]{2,0,1:T(1,128)} %copy-done.34) | copy-start | bytes 6148
  513.2 21.0 %copy-start.37 = (f32[1,1,512]{2,0,1:T(1,128)S(1)}, f32[1,1,512]{2,0,1:T(1,128)}, u32[]{:S(2)}) copy-start(f32[1,1,512]{2,0,1:T(1,128)} %copy-done.36) | copy-start | bytes 6148
  513.2 21.0 %copy-start.38 = (f32[1,1,512]{2,0,1:T(1,128)S(1)}, f32[1,1,512]{2,0,1:T(1,128)}, u32[]{:S(2)}) copy-start(f32[1,1,512]{2,0,1:T(1,128)} %get-tuple-element.58) | copy-start | bytes 6148
  513.2 21.0 %copy-start.40 = (f32[1,1,512]{2,0,1:T(1,128)S(1)}, f32[1,1,512]{2,0,1:T(1,128)}, u32[]{:S(2)}) copy-start(f32[1,1,512]{2,0,1:T(1,128)} %copy-done.39) | copy-start | bytes 6148
  513.2 21.0 %copy-start.41 = (f32[1,1,512]{2,0,1:T(1,128)S(1)}, f32[1,1,512]{2,0,1:T(1,128)}, u32[]{:S(2)}) copy-start(f32[1,1,512]{2,0,1:T(1,128)} %get-tuple-element.55) | copy-start | bytes 6148
  513.2 21.0 %copy-start.43 = (f32[1,1,512]{2,0,1:T(1,128)S(1)}, f32[1,1,512]{2,0,1:T(1,128)}, u32[]{:S(2)}) copy-start(f32[1,1,512]{2,0,1:T(1,128)} %copy-done.42) | copy-start | bytes 6148
  513.3 21.0 %copy-start.44 = (f32[1,1,512]{2,0,1:T(1,128)S(1)}, f32[1,1,512]{2,0,1:T(1,128)}, u32[]{:S(2)}) copy-start(f32[1,1,512]{2,0,1:T(1,128)} %get-tuple-element.52) | copy-start | bytes 6148
  513.3 21.0 %copy-start.46 = (f32[1,1,512]{2,0,1:T(1,128)S(1)}, f32[1,1,512]{2,0,1:T(1,128)}, u32[]{:S(2)}) copy-start(f32[1,1,512]{2,0,1:T(1,128)} %copy-done.45) | copy-start | bytes 6148
  513.3 21.0 %copy-start.49 = (f32[1,1,512]{2,0,1:T(1,128)S(1)}, f32[1,1,512]{2,0,1:T(1,128)}, u32[]{:S(2)}) copy-start(f32[1,1,512]{2,0,1:T(1,128)} %copy-done.48) | copy-start | bytes 6148
  513.3 21.0 %copy-start.50 = (f32[1,1,512]{2,0,1:T(1,128)S(1)}, f32[1,1,512]{2,0,1:T(1,128)}, u32[]{:S(2)}) copy-start(f32[1,1,512]{2,0,1:T(1,128)} %get-tuple-element.49) | copy-start | bytes 6148
  513.3 21.0 %copy-start.52 = (s32[512]{0:T(512)S(1)}, s32[512]{0:T(512)}, u32[]{:S(2)}) copy-start(s32[512]{0:T(512)} %copy-done.51) | copy-start | bytes 6148
  513.3 21.0 %copy-start.54 = (s32[512]{0:T(512)S(1)}, s32[512]{0:T(512)}, u32[]{:S(2)}) copy-start(s32[512]{0:T(512)} %copy-done.53) | copy-start | bytes 6148
  513.3 21.0 %copy-start.56 = (s32[512]{0:T(512)S(1)}, s32[512]{0:T(512)}, u32[]{:S(2)}) copy-start(s32[512]{0:T(512)} %copy-done.55) | copy-start | bytes 6148
  513.3 21.0 %copy-start.58 = (s32[512]{0:T(512)S(1)}, s32[512]{0:T(512)}, u32[]{:S(2)}) copy-start(s32[512]{0:T(512)} %copy-done.57) | copy-start | bytes 6148
  513.3 21.0 %copy-start.60 = (s32[512]{0:T(512)S(1)}, s32[512]{0:T(512)}, u32[]{:S(2)}) copy-start(s32[512]{0:T(512)} %copy-done.59) | copy-start | bytes 6148
  513.3 21.0 %copy-start.62 = (s32[512]{0:T(512)S(1)}, s32[512]{0:T(512)}, u32[]{:S(2)}) copy-start(s32[512]{0:T(512)} %copy-done.61) | copy-start | bytes 6148
  521.3 12.5 %collective-permute-start.2 = (f32[5,12,384]{2,0,1:T(8,128)S(1)}, f32[5,12,384]{2,0,1:T(8,128)S(1)}, u32[]{:S(2)}, u32[]{:S(2)}) collective-permute-start(f32[5,12,384]{2,0,1:T(8,128)S(1)} %slice.412), channel_id=1, source_target_pairs={{0,224},{32,0},{64,32},{96,64},{128,96},{160,128},{192,160},{224,1... | collective-permute-start | bytes 276488 | tf_op jit(solution)/shard_map/ppermute | solution.py:20
  533.8 15.1 %collective-permute-start.3 = (f32[53,5,384]{2,0,1:T(8,128)S(1)}, f32[53,5,384]{2,0,1:T(8,128)S(1)}, u32[]{:S(2)}, u32[]{:S(2)}) collective-permute-start(f32[53,5,384]{2,0,1:T(8,128)S(1)} %pad_maximum_fusion.5), channel_id=1, source_target_pairs={{0,31},{1,0},{2,1},{3,2},{4,3},{5,4},{6,5},{7,6},{8,7},{9,8},{10,9... | collective-permute-start | bytes 1221128 | tf_op jit(solution)/shard_map/ppermute | solution.py:20
  (21 other events, 68.0 us)
where the time goes:
time: 578 us; the launch traced here: 569 us
  local copies, waits for them, and re-layouts  169 us (29%)
  matrix products  118 us (20%)
  blocking collectives  116 us (20%)
  waiting for transfers between devices  79.1 us (14%)
  starting transfers between devices  47.4 us (8%)
  other arithmetic  36.2 us (6%)
    dot_general x20, matrix products, multiply(): jnp.einsum(pattern, operand, table, precision=PRECISE, preferred_element_...  106 us
    unnamed x136, local copies, waits for them, and re-layouts  78.5 us
    all_to_all x2, blocking collectives, columns_py(): return lax.all_to_all(layers, 'py', split_axis=2, concat_axis=3, tiled=True)  71.8 us
    all_to_all x1, blocking collectives, columns_px(): return lax.all_to_all(layers, 'px', split_axis=2, concat_axis=3, tiled=True)  44.4 us
    ppermute x4, waiting for transfers between devices, from_behind(): return lax.ppermute(value, axis, pairs)  39.8 us
    all_to_all x1, waiting for transfers between devices, columns_px(): return lax.all_to_all(layers, 'px', split_axis=2, concat_axis=3, tiled=True)  39.3 us
    all_to_all x1, starting transfers between devices, columns_px(): return lax.all_to_all(layers, 'px', split_axis=2, concat_axis=3, tiled=True)  39.2 us
    another operation x3, local copies, waits for them, and re-layouts, transform(): return jnp.stack([real_part, imag_part])  16 us
  transfers between devices with their start and end apart: 5, of which 5 were waited for; matrix products, arithmetic and copies ran while one was open for 1% of the time, Pallas kernels for 0%

commit v1 on v0

v1 whole, which is shorter than its diff:
```python
import math

import jax
import jax.numpy as jnp
import ml_dtypes
import numpy as np
from jax import lax
from jax.experimental import pallas as pl
from jax.experimental.pallas import tpu as pltpu
from jax.sharding import PartitionSpec as P

GRID = 384
ORDER = 6
SLOTS = 512
N_PX = 8
N_PY = 32
COUNT = N_PX * N_PY
WIDE_X = GRID // N_PX
WIDE_Y = GRID // N_PY
CELLS = WIDE_X * WIDE_Y
LINES = GRID // 2 + 1
HALF = 64
LANES = 128
CHUNKS = CELLS // HALF
ROWS = 208
PADDED = 256
EDGE_X = 16
EDGE_Y = 5
SPLITTING = 1.6
COUPLING = 1.0 / math.pi
MESH = pl.DeviceIdType.MESH
NT = (((1,), (1,)), ((), ()))
NN = (((1,), (0,)), ((), ()))
CLASSES = ((0, 0, WIDE_X, WIDE_Y), (0, 1, WIDE_X, EDGE_Y), (1, 0, EDGE_X, WIDE_Y), (1, 1, EDGE_X, EDGE_Y))


def halves(table):
    high = table.astype(ml_dtypes.bfloat16)
    low = (table - high.astype(np.float64)).astype(ml_dtypes.bfloat16)
    return high, low


def chunked(first, second):
    rows = first.shape[0]
    pair = np.stack([first.reshape(rows, CHUNKS, HALF), second.reshape(rows, CHUNKS, HALF)], axis=2)
    return np.ascontiguousarray(pair.reshape(rows, CHUNKS, LANES).transpose(1, 0, 2))


def turn(numerators, period):
    return 2.0 * math.pi / period * np.mod(numerators, period).astype(np.float64)


def line_table():
    at = np.arange(GRID)
    angles = turn(np.arange(LINES)[:, None] * at[None, :], GRID)
    table = np.zeros((2, PADDED, GRID))
    table[0, :LINES] = np.cos(angles)
    table[1, :LINES] = -np.sin(angles)
    return table.reshape(2 * PADDED, GRID)


def brick_table():
    device = np.arange(COUNT)
    a, b = device // N_PY, device % N_PY
    angles = turn(4 * a[:, None] * a[None, :] + b[:, None] * b[None, :], N_PY)
    return np.concatenate([np.cos(angles), -np.sin(angles)])


def twiddle_tables():
    device = np.arange(COUNT)
    cell = np.arange(CELLS)
    a, b = device // N_PY, device % N_PY
    y, x = cell // WIDE_X, cell % WIDE_X
    angles = turn(a[:, None] * x[None, :] + b[:, None] * y[None, :], GRID)
    cosines, sines = np.cos(angles), -np.sin(angles)
    return chunked(cosines, cosines), chunked(-sines, sines)


def cell_table():
    cell = np.arange(CELLS)
    y, x = cell // WIDE_X, cell % WIDE_X
    angles = turn(4 * y[:, None] * y[None, :] + x[:, None] * x[None, :], WIDE_X)
    cosines, sines = np.cos(angles), -np.sin(angles)
    table = np.zeros((CHUNKS, 2, HALF, CHUNKS, 2, HALF))
    shape = (CHUNKS, HALF, CHUNKS, HALF)
    table[:, 0, :, :, 0, :] = cosines.reshape(shape)
    table[:, 0, :, :, 1, :] = sines.reshape(shape)
    table[:, 1, :, :, 0, :] = -sines.reshape(shape)
    table[:, 1, :, :, 1, :] = cosines.reshape(shape)
    return table.reshape(2 * CELLS, 2 * CELLS)


def axis_terms(indices):
    signed = np.where(indices <= GRID // 2, indices, indices - GRID) / GRID
    values = [1.0, 0.0]
    for k in range(2, ORDER):
        values = [
            ((k - j) * (values[j - 1] if j >= 1 else 0.0) + (1.0 + j) * (values[j] if j < k else 0.0)) / k
            for j in range(k + 1)
        ]
    total = sum(values[j] * np.exp(1j * turn(indices * j, GRID)) for j in range(ORDER - 1))
    return signed * signed, 1.0 / np.abs(total) ** 2


def green_tables():
    device = np.arange(COUNT)
    cell = np.arange(CELLS)
    freq_x = (device // N_PY)[:, None] + N_PX * (cell % WIDE_X)[None, :]
    freq_y = (device % N_PY)[:, None] + N_PY * (cell // WIDE_X)[None, :]
    square_x, modulus_x = axis_terms(freq_x)
    square_y, modulus_y = axis_terms(freq_y)
    squares = square_x + square_y
    rate = math.pi * math.pi / (SPLITTING * SPLITTING)
    gains = np.exp(-rate * squares) * modulus_x * modulus_y
    square_z, modulus_z = axis_terms(np.arange(LINES))
    weight = np.full(LINES, 2.0)
    weight[0] = weight[-1] = 1.0
    factor = COUPLING / float(GRID) ** 3
    line = np.zeros((ROWS, 2, LANES))
    line[:LINES, 0] = square_z[:, None]
    line[:LINES, 1] = (factor * weight * np.exp(-rate * square_z) * modulus_z)[:, None]
    return chunked(squares, squares), chunked(gains, -gains), line.reshape(ROWS, 2 * LANES)


def split(value):
    high = value.astype(jnp.bfloat16)
    return high, (value - high.astype(jnp.float32)).astype(jnp.bfloat16)


def product(left, right, dims):
    def one(a, b):
        return lax.dot_general(a, b, dims, preferred_element_type=jnp.float32)

    return one(left[0], right[0]) + one(left[0], right[1]) + one(left[1], right[0])


def spline_rows(fraction):
    values = [1.0 - fraction, fraction]
    previous = values
    for k in range(2, ORDER):
        previous = values
        updated = []
        for j in range(k + 1):
            terms = []
            if j >= 1:
                terms.append((fraction + float(k - j)) * previous[j - 1])
            if j < k:
                terms.append((float(1 + j) - fraction) * previous[j])
            updated.append(sum(terms[1:], terms[0]) * (1.0 / k))
        values = updated
    slopes = []
    for j in range(ORDER):
        if j == 0:
            slopes.append(-previous[0])
        elif j == ORDER - 1:
            slopes.append(previous[j - 1])
        else:
            slopes.append(previous[j - 1] - previous[j])
    return values, slopes


def place(offset, rows):
    total = jnp.zeros(offset.shape, jnp.float32)
    for j in range(ORDER):
        total = jnp.where(offset == j, rows[j], total)
    return total


def swap(value):
    return pltpu.roll(value, HALF, 1)


def kernel(
    charges,
    cells,
    fractions,
    filled,
    line_hi_any,
    line_lo_any,
    brick_hi_any,
    brick_lo_any,
    cell_hi_any,
    cell_lo_any,
    twiddle_any,
    green_any,
    line_green,
    potential_out,
    force_out,
    line_hi,
    line_lo,
    brick_hi,
    brick_lo,
    cell_hi,
    cell_lo,
    twiddle,
    green,
    atoms,
    wx,
    sx,
    wy,
    sy,
    wz_hi,
    wz_lo,
    column_hi,
    column_lo,
    grid,
    outbound,
    inbound,
    multiplier,
    first_hi,
    first_lo,
    second_hi,
    second_lo,
    returning,
    returned,
    turned_hi,
    turned_lo,
    field_hi,
    field_lo,
    sampled,
    partials,
    received,
    table_sems,
    atom_send,
    atom_recv,
    out_send,
    out_recv,
    back_send,
    back_recv,
    part_send,
    part_recv,
):
    px = lax.axis_index("px")
    py = lax.axis_index("py")
    me = px * N_PY + py

    barrier = pltpu.get_barrier_semaphore()

    def greet(step, carry):
        other = lax.rem(me + step, COUNT)
        pl.semaphore_signal(barrier, inc=1, device_id=(other // N_PY, lax.rem(other, N_PY)), device_id_type=MESH)
        return carry

    lax.fori_loop(1, COUNT, greet, 0)

    tables = [
        pltpu.make_async_copy(source, target, table_sems.at[number])
        for number, (source, target) in enumerate(
            [
                (line_hi_any, line_hi),
                (line_lo_any, line_lo),
                (brick_hi_any, brick_hi),
                (brick_lo_any, brick_lo),
                (twiddle_any, twiddle),
                (green_any, green),
                (cell_hi_any, cell_hi),
                (cell_lo_any, cell_lo),
            ]
        )
    ]
    for table in tables:
        table.start()

    slot = lax.broadcasted_iota(jnp.int32, (1, SLOTS), 1)
    occupied = (slot < filled[...]).astype(jnp.float32)
    weighted = charges[0] * occupied
    atoms[0, 0:1] = weighted
    for d in range(3):
        atoms[0, 1 + d : 2 + d] = cells[d, 0].astype(jnp.float32)
        atoms[0, 4 + d : 5 + d] = fractions[d, 0]
    atoms[0, 7:8] = jnp.zeros((1, SLOTS), jnp.float32)
    returned[:, LINES - 1 :, :] = jnp.zeros((CHUNKS, PADDED - LINES + 1, LANES), jnp.float32)

    def side_tables(number):
        step_x, step_y, size_x, size_y = CLASSES[number]
        values, slopes = spline_rows(atoms[number, 4:7])
        for row, step, wide, size, weights, rises in (
            (0, step_x, WIDE_X, size_x, wx, sx),
            (1, step_y, WIDE_Y, 16, wy, sy),
        ):
            start = atoms[number, 1 + row : 2 + row].astype(jnp.int32) - step * wide
            offset = lax.broadcasted_iota(jnp.int32, (size, SLOTS), 0) - start
            weights[number, :size] = place(offset, [v[row : row + 1] for v in values])
            rises[number, :size] = place(offset, [v[row : row + 1] for v in slopes])

    def depth_tables(number, kind):
        rows = [v[2:3] for v in spline_rows(atoms[number, 4:7])[kind]]
        start = atoms[number, 3:4].astype(jnp.int32)
        lanes = pl.ds((2 * number + kind) * SLOTS, SLOTS)

        def block(step, carry):
            at = pl.multiple_of(step * 16, 16)
            offset = lax.broadcasted_iota(jnp.int32, (16, SLOTS), 0) + at - start
            offset = jnp.where(offset < 0, offset + GRID, offset)
            high, low = split(place(offset, rows))
            wz_hi[pl.ds(at, 16), lanes] = high
            wz_lo[pl.ds(at, 16), lanes] = low
            return carry

        lax.fori_loop(0, GRID // 16, block, 0)

    def spread(number):
        size_x, size_y = CLASSES[number][2:]
        charged = wx[number, :size_x] * atoms[number, 0:1]
        for k in range(size_y):
            high, low = split(charged * wy[number, k : k + 1])
            column_hi[k * size_x : (k + 1) * size_x] = high
            column_lo[k * size_x : (k + 1) * size_x] = low
        lanes = pl.ds(2 * number * SLOTS, SLOTS)
        total = size_x * size_y
        return product((column_hi[:total], column_lo[:total]), (wz_hi[:, lanes], wz_lo[:, lanes]), NT)

    side_tables(0)
    depth_tables(0, 0)

    pl.semaphore_wait(barrier, COUNT - 1)

    atom_copies = []
    for number in range(1, 4):
        step_x, step_y = CLASSES[number][:2]
        target = (lax.rem(px + step_x, N_PX), lax.rem(py + step_y, N_PY))
        copy = pltpu.make_async_remote_copy(
            atoms.at[0], atoms.at[number], atom_send.at[number], atom_recv.at[number], device_id=target, device_id_type=MESH
        )
        copy.start()
        atom_copies.append(copy)

    grid[:CELLS] = spread(0)
    grid[CELLS:] = jnp.zeros((CHUNKS * HALF + HALF - CELLS, GRID), jnp.float32)
    for number in range(1, 4):
        atom_copies[number - 1].wait_recv()
        side_tables(number)
        depth_tables(number, 0)
        size_x, size_y = CLASSES[number][2:]
        added = spread(number)
        for k in range(size_y):
            grid[k * WIDE_X : k * WIDE_X + size_x] += added[k * size_x : (k + 1) * size_x]

    tables[0].wait()
    tables[1].wait()
    dense = split(grid[...])
    cosine_part = product((line_hi[:ROWS], line_lo[:ROWS]), dense, NT)
    sine_part = product((line_hi[PADDED : PADDED + ROWS], line_lo[PADDED : PADDED + ROWS]), dense, NT)
    lower = lax.broadcasted_iota(jnp.int32, (ROWS, LANES), 1) < HALF
    for j in range(CHUNKS):
        at = (j // 2) * LANES
        cosine_block = cosine_part[:, at : at + LANES]
        sine_block = sine_part[:, at : at + LANES]
        if j % 2 == 0:
            outbound[j] = jnp.where(lower, cosine_block, swap(sine_block))
        else:
            outbound[j] = jnp.where(lower, swap(cosine_block), sine_block)

    def send_line(line, to_x, to_y):
        mine = jnp.logical_and(to_x == px, to_y == py)

        @pl.when(mine)
        def _():
            pltpu.make_async_copy(outbound.at[:, pl.ds(line, 1), :], inbound.at[:, pl.ds(me, 1), :], out_recv).start()

        @pl.when(jnp.logical_not(mine))
        def _():
            pltpu.make_async_remote_copy(
                outbound.at[:, pl.ds(line, 1), :],
                inbound.at[:, pl.ds(me, 1), :],
                out_send,
                out_recv,
                device_id=(to_x, to_y),
                device_id_type=MESH,
            ).start()

    def send_even(step, carry):
        line = lax.rem(step + me, 128)
        send_line(line, 2 * (line // N_PY), lax.rem(line, N_PY))
        return carry

    def send_odd(step, carry):
        line = lax.rem(step + me, 64)
        depth = line // 16
        pair = 2 * lax.rem(line, 16)
        send_line(128 + line, 2 * depth + 1, pair + lax.rem(depth + pair // 4, 2))
        return carry

    lax.fori_loop(0, 128, send_even, 0)
    lax.fori_loop(0, 64, send_odd, 0)
    send_line(LINES - 1, 1, 1)

    odd = lax.rem(px, 2)
    depth = px // 2
    order = depth * N_PY + py
    last = jnp.logical_and(px == 1, py == 1)
    matching = lax.rem(depth + py // 4 + py, 2) == 0
    active = jnp.logical_or(jnp.logical_or(odd == 0, last), matching)
    line_me = (1 - odd) * order + odd * (128 + order // 2)
    line_me = line_me + last.astype(jnp.int32) * (LINES - 1 - 128)

    for number in range(4):
        depth_tables(number, 1)
    for table in tables[2:]:
        table.wait()

    def wait_rows(buffer, count, semaphore):
        view = buffer.at[:, pl.ds(0, count), :]
        pltpu.make_async_copy(view, view, semaphore).wait()

    @pl.when(active)
    def _():
        scalars = line_green[pl.ds(line_me, 1), :]
        square_z = scalars[:, :LANES]
        gain_z = scalars[:, LANES:]
        for j in range(CHUNKS):
            squared = green[0, j] + square_z
            positive = squared > 0.0
            bounded = jnp.where(positive, squared, 1.0)
            multiplier[j] = jnp.where(positive, green[1, j] * gain_z / bounded, 0.0)

        wait_rows(inbound, COUNT, out_recv)
        left = lax.broadcasted_iota(jnp.int32, (COUNT, LANES), 1) < HALF
        groups = [(0, 2), (2, 4), (4, 6), (6, 8), (8, 9)]
        brick_pair = (brick_hi[...], brick_lo[...])

        def turned(value, j):
            return value * twiddle[0, j] + swap(value) * twiddle[1, j]

        for begin, end in groups:
            block = jnp.concatenate([inbound[j] for j in range(begin, end)], axis=1)
            mixed = product(brick_pair, split(block), NN)
            for j in range(begin, end):
                at = (j - begin) * LANES
                upper = mixed[:COUNT, at : at + LANES]
                crossed = swap(mixed[COUNT:, at : at + LANES])
                value = upper + jnp.where(left, -crossed, crossed)
                high, low = split(turned(value, j))
                first_hi[:, j * LANES : (j + 1) * LANES] = high
                first_lo[:, j * LANES : (j + 1) * LANES] = low
        for begin, end in groups:
            lanes = slice(begin * LANES, end * LANES)
            block = product((first_hi[...], first_lo[...]), (cell_hi[:, lanes], cell_lo[:, lanes]), NN)
            for j in range(begin, end):
                at = (j - begin) * LANES
                high, low = split(block[:, at : at + LANES] * multiplier[j])
                second_hi[:, j * LANES : (j + 1) * LANES] = high
                second_lo[:, j * LANES : (j + 1) * LANES] = low
        for begin, end in groups:
            lanes = slice(begin * LANES, end * LANES)
            block = product((second_hi[...], second_lo[...]), (cell_hi[:, lanes], cell_lo[:, lanes]), NN)
            block = jnp.concatenate(
                [turned(block[:, (j - begin) * LANES : (j - begin + 1) * LANES], j) for j in range(begin, end)], axis=1
            )
            mixed = product(brick_pair, split(block), NN)
            for j in range(begin, end):
                at = (j - begin) * LANES
                upper = mixed[:COUNT, at : at + LANES]
                crossed = swap(mixed[COUNT:, at : at + LANES])
                returning[j] = jnp.where(left, upper, -upper) - crossed

        def send_back(step, carry):
            other = lax.rem(me + step, COUNT)
            pltpu.make_async_remote_copy(
                returning.at[:, pl.ds(other, 1), :],
                returned.at[:, pl.ds(line_me, 1), :],
                back_send,
                back_recv,
                device_id=(other // N_PY, lax.rem(other, N_PY)),
                device_id_type=MESH,
            ).start()
            return carry

        pltpu.make_async_copy(returning.at[:, pl.ds(me, 1), :], returned.at[:, pl.ds(line_me, 1), :], back_recv).start()
        lax.fori_loop(1, COUNT, send_back, 0)

    wait_rows(returned, LINES, back_recv)
    for j in range(CHUNKS):
        high, low = split(returned[j].T)
        rows = slice(j * HALF, (j + 1) * HALF)
        turned_hi[rows, :PADDED] = high[:HALF]
        turned_hi[rows, PADDED:] = high[HALF:]
        turned_lo[rows, :PADDED] = low[:HALF]
        turned_lo[rows, PADDED:] = low[HALF:]
    high, low = split(product((turned_hi[...], turned_lo[...]), (line_hi[...], line_lo[...]), NN))
    field_hi[...] = high
    field_lo[...] = low

    def sample(number):
        size_x, size_y = CLASSES[number][2:]
        total = size_x * size_y
        if size_x == WIDE_X:
            field = (field_hi[:total], field_lo[:total])
        else:
            field = tuple(
                jnp.concatenate([part[k * WIDE_X : k * WIDE_X + size_x] for k in range(size_y)], axis=0)
                for part in (field_hi, field_lo)
            )
        lanes = slice(2 * number * SLOTS, 2 * (number + 1) * SLOTS)
        sampled[:total] = product(field, (wz_hi[:, lanes], wz_lo[:, lanes]), NN)

        def block(step, carry):
            at = pl.multiple_of(step * LANES, LANES)
            here = pl.ds(at, LANES)
            over_y = jnp.zeros((size_x, LANES), jnp.float32)
            slope_over_y = over_y
            rising_over_y = over_y
            for k in range(size_y):
                rows = slice(k * size_x, (k + 1) * size_x)
                level = sampled[rows, here]
                rising = sampled[rows, pl.ds(SLOTS + at, LANES)]
                weight = wy[number, k : k + 1, here]
                over_y += weight * level
                slope_over_y += sy[number, k : k + 1, here] * level
                rising_over_y += weight * rising
            weight = wx[number, :size_x, here]
            partials[number, 0:1, here] = jnp.sum(weight * over_y, axis=0, keepdims=True)
            partials[number, 1:2, here] = jnp.sum(sx[number, :size_x, here] * over_y, axis=0, keepdims=True)
            partials[number, 2:3, here] = jnp.sum(weight * slope_over_y, axis=0, keepdims=True)
            partials[number, 3:4, here] = jnp.sum(weight * rising_over_y, axis=0, keepdims=True)
            return carry

        lax.fori_loop(0, SLOTS // LANES, block, 0)

    part_copies = []
    for number in range(1, 4):
        sample(number)
        step_x, step_y = CLASSES[number][:2]
        target = (lax.rem(px + N_PX - step_x, N_PX), lax.rem(py + N_PY - step_y, N_PY))
        copy = pltpu.make_async_remote_copy(
            partials.at[number],
            received.at[number],
            part_send.at[number],
            part_recv.at[number],
            device_id=target,
            device_id_type=MESH,
        )
        copy.start()
        part_copies.append(copy)
    sample(0)
    summed = partials[0, 0:4]
    for number in range(1, 4):
        part_copies[number - 1].wait_recv()
        summed = summed + received[number, 0:4]
    potential_out[0] = summed[0:1] * occupied
    for d in range(3):
        force_out[d, 0] = -weighted * summed[1 + d : 2 + d]

    for copy in atom_copies + part_copies:
        copy.wait_send()

    @pl.when(active)
    def _():
        wait_rows(outbound, LINES - 1, out_send)
        wait_rows(returning, COUNT - 1, back_send)

    @pl.when(jnp.logical_not(active))
    def _():
        wait_rows(outbound, LINES, out_send)


def shards(charges, cells, fractions, filled):
    line = halves(line_table())
    brick = halves(brick_table())
    cell = halves(cell_table())
    twiddle = np.stack(twiddle_tables()).astype(np.float32)
    squares, gains, line_green = green_tables()
    green = np.stack([squares, gains]).astype(np.float32)
    constants = [*line, *brick, *cell, twiddle, green, line_green.astype(np.float32)]
    f32, bf16 = jnp.float32, jnp.bfloat16
    vmem = pltpu.VMEM
    message = vmem((CHUNKS, COUNT, LANES), f32)
    plane = vmem((COUNT, 2 * CELLS), bf16)
    whole = pl.BlockSpec(memory_space=pltpu.VMEM)
    distant = pl.BlockSpec(memory_space=pl.ANY)
    return pl.pallas_call(
        kernel,
        out_shape=(jax.ShapeDtypeStruct((1, 1, SLOTS), f32), jax.ShapeDtypeStruct((3, 1, 1, SLOTS), f32)),
        in_specs=[whole] * 4 + [distant] * 8 + [whole],
        out_specs=(whole, whole),
        scratch_shapes=[
            vmem((2 * PADDED, GRID), bf16),
            vmem((2 * PADDED, GRID), bf16),
            vmem((2 * COUNT, COUNT), bf16),
            vmem((2 * COUNT, COUNT), bf16),
            vmem((2 * CELLS, 2 * CELLS), bf16),
            vmem((2 * CELLS, 2 * CELLS), bf16),
            vmem((2, CHUNKS, COUNT, LANES), f32),
            vmem((2, CHUNKS, COUNT, LANES), f32),
            vmem((4, 8, SLOTS), f32),
            vmem((4, WIDE_X, SLOTS), f32),
            vmem((4, WIDE_X, SLOTS), f32),
            vmem((4, 16, SLOTS), f32),
            vmem((4, 16, SLOTS), f32),
            vmem((GRID, 8 * SLOTS), bf16),
            vmem((GRID, 8 * SLOTS), bf16),
            vmem((CELLS, SLOTS), bf16),
            vmem((CELLS, SLOTS), bf16),
            vmem((CELLS + HALF, GRID), f32),
            vmem((CHUNKS, ROWS, LANES), f32),
            message,
            message,
            plane,
            plane,
            plane,
            plane,
            message,
            message,
            vmem((CELLS, 2 * PADDED), bf16),
            vmem((CELLS, 2 * PADDED), bf16),
            vmem((CELLS, GRID), bf16),
            vmem((CELLS, GRID), bf16),
            vmem((CELLS, 2 * SLOTS), f32),
            vmem((4, 8, SLOTS), f32),
            vmem((4, 8, SLOTS), f32),
            pltpu.SemaphoreType.DMA((8,)),
            pltpu.SemaphoreType.DMA((4,)),
            pltpu.SemaphoreType.DMA((4,)),
            pltpu.SemaphoreType.DMA,
            pltpu.SemaphoreType.DMA,
            pltpu.SemaphoreType.DMA,
            pltpu.SemaphoreType.DMA,
            pltpu.SemaphoreType.DMA((4,)),
            pltpu.SemaphoreType.DMA((4,)),
        ],
        compiler_params=pltpu.CompilerParams(
            collective_id=0, has_side_effects=True, vmem_limit_bytes=56 * 1024 * 1024
        ),
    )(charges, cells, fractions, filled, *[jnp.asarray(table) for table in constants])


def solution(mesh):
    placed = (
        P("px", "py", None),
        P(None, "px", "py", None),
        P(None, "px", "py", None),
        P("px", "py"),
    )
    return jax.shard_map(
        shards,
        mesh=mesh,
        in_specs=placed,
        out_specs=(P("px", "py", None), P(None, "px", "py", None)),
        check_vma=False,
    )
```

time: 578 us -> 102 us (0.18)
  the two profiles are of different devices: /device:TPU:1 before, /device:TPU:63 now
where the time goes in v1:
time: 102 us
  Pallas kernels  97.9 us (96%)
  local copies, waits for them, and re-layouts  2.52 us (2%)
  between operations  1.29 us (1%)
    pallas_call x1, Pallas kernels, shards(): pl.pallas_call(kernel, out_shape=(jax.ShapeDtypeStruct((1, 1, SLOTS), f32...  97.9 us
    unnamed x2, local copies, waits for them, and re-layouts  2.52 us

profile of v1, /device:TPU:63, one launch (start us, length us, event | category | flops | bytes accessed | tf_op | source)
XLA Modules:
  0.0 101.7 jit_solution(10958617679121599313)
XLA Ops:
  1.3 97.9 %shard_map.140 = (f32[1,1,512]{2,1,0:T(1,128)}, f32[3,1,1,512]{3,2,1,0:T(1,128)}) custom-call(f32[1,1,512]{2,1,0:T(1,128)} %charges.1, s32[3,1,1,512]{3,2,1,0:T(1,128)} %cells.1, f32[3,1,1,512]{3,2,1,0:T(1,128)} %fractions.1, s32[1,1]{1,0:T(1,128)S(6)} %copy.17.filled, bf16[512,384]{1,0:T(8,128)(2,1)} %constant.18.clone.line_hi_any, ...), custom_call_target="tpu_custom_call" | custom-call | tf_op jit(solution)/shard_map/pallas_call | solution.py:571
  99.1 1.2 %copy.18 = f32[1,1,512]{2,1,0:T(1,128)} copy(f32[1,1,512]{2,1,0:T(1,128)} %get-tuple-element.4) | data formatting | bytes 4096
  100.4 1.3 %copy.19 = f32[3,1,1,512]{3,2,1,0:T(1,128)} copy(f32[3,1,1,512]{3,2,1,0:T(1,128)} %get-tuple-element.5) | data formatting | bytes 12288

commit v2 on v1

--- a/solution.py
+++ b/solution.py
@@ -31,6 +31,7 @@
 MESH = pl.DeviceIdType.MESH
 NT = (((1,), (1,)), ((), ()))
 NN = (((1,), (0,)), ((), ()))
+GROUPS = ((0, 6, 0, 8), (6, 9, 8, 12))
 CLASSES = ((0, 0, WIDE_X, WIDE_Y), (0, 1, WIDE_X, EDGE_Y), (1, 0, EDGE_X, WIDE_Y), (1, 1, EDGE_X, EDGE_Y))
 
 
@@ -131,7 +132,9 @@
     def one(a, b):
         return lax.dot_general(a, b, dims, preferred_element_type=jnp.float32)
 
-    return one(left[0], right[0]) + one(left[0], right[1]) + one(left[1], right[0])
+    rows = left[0].shape[0]
+    both = one(jnp.concatenate([left[0], left[1]], axis=0), right[0])
+    return both[:rows] + both[rows:] + one(left[0], right[1])
 
 
 def spline_rows(fraction):
@@ -184,8 +187,7 @@
     twiddle_any,
     green_any,
     line_green,
-    potential_out,
-    force_out,
+    result,
     line_hi,
     line_lo,
     brick_hi,
@@ -217,6 +219,8 @@
     turned_lo,
     field_hi,
     field_lo,
+    spectrum,
+    rises_z,
     sampled,
     partials,
     received,
@@ -229,6 +233,7 @@
     back_recv,
     part_send,
     part_recv,
+    vouched,
 ):
     px = lax.axis_index("px")
     py = lax.axis_index("py")
@@ -236,12 +241,21 @@
 
     barrier = pltpu.get_barrier_semaphore()
 
-    def greet(step, carry):
-        other = lax.rem(me + step, COUNT)
-        pl.semaphore_signal(barrier, inc=1, device_id=(other // N_PY, lax.rem(other, N_PY)), device_id_type=MESH)
+    def greet(target):
+        pl.semaphore_signal(barrier, inc=1, device_id=target, device_id_type=MESH)
+
+    def greet_row(step, carry):
+        greet((px, lax.rem(py + step, N_PY)))
         return carry
 
-    lax.fori_loop(1, COUNT, greet, 0)
+    def greet_column(step, carry):
+        greet((lax.rem(px + step, N_PX), py))
+        return carry
+
+    greet((lax.rem(px + 1, N_PX), lax.rem(py + 1, N_PY)))
+    greet((lax.rem(px + N_PX - 1, N_PX), lax.rem(py + N_PY - 1, N_PY)))
+    lax.fori_loop(1, N_PX, greet_column, 0)
+    lax.fori_loop(1, N_PY, greet_row, 0)
 
     tables = [
         pltpu.make_async_copy(source, target, table_sems.at[number])
@@ -283,37 +297,50 @@
             weights[number, :size] = place(offset, [v[row : row + 1] for v in values])
             rises[number, :size] = place(offset, [v[row : row + 1] for v in slopes])
 
-    def depth_tables(number, kind):
-        rows = [v[2:3] for v in spline_rows(atoms[number, 4:7])[kind]]
+    def depth_block(start, rows, at, lanes):
+        offset = lax.broadcasted_iota(jnp.int32, (16, SLOTS), 0) + at - start
+        offset = jnp.where(offset < 0, offset + GRID, offset)
+        high, low = split(place(offset, rows))
+        wz_hi[pl.ds(at, 16), lanes] = high
+        wz_lo[pl.ds(at, 16), lanes] = low
+
+    def depth_tables(number):
+        values, slopes = spline_rows(atoms[number, 4:7])
+        rows = [v[2:3] for v in values]
         start = atoms[number, 3:4].astype(jnp.int32)
-        lanes = pl.ds((2 * number + kind) * SLOTS, SLOTS)
+        for j in range(ORDER):
+            rises_z[number, j : j + 1] = slopes[j][2:3]
 
         def block(step, carry):
-            at = pl.multiple_of(step * 16, 16)
-            offset = lax.broadcasted_iota(jnp.int32, (16, SLOTS), 0) + at - start
-            offset = jnp.where(offset < 0, offset + GRID, offset)
-            high, low = split(place(offset, rows))
-            wz_hi[pl.ds(at, 16), lanes] = high
-            wz_lo[pl.ds(at, 16), lanes] = low
+            depth_block(start, rows, pl.multiple_of(step * 16, 16), pl.ds(2 * number * SLOTS, SLOTS))
             return carry
 
         lax.fori_loop(0, GRID // 16, block, 0)
 
-    def spread(number):
-        size_x, size_y = CLASSES[number][2:]
+    def slope_block(step):
+        step = jnp.minimum(step, 4 * GRID // 32 - 1)
+        number = lax.div(step, GRID // 32)
+        at = lax.rem(step, GRID // 32) * 32
+        rows = [rises_z[number, j : j + 1] for j in range(ORDER)]
+        start = atoms[number, 3:4].astype(jnp.int32)
+        lanes = pl.ds(pl.multiple_of((2 * number + 1) * SLOTS, SLOTS), SLOTS)
+        for k in range(2):
+            depth_block(start, rows, pl.multiple_of(at + 16 * k, 16), lanes)
+
+    def spread(number, begin, end):
+        size_x = CLASSES[number][2]
+        end = min(end, CLASSES[number][3])
         charged = wx[number, :size_x] * atoms[number, 0:1]
-        for k in range(size_y):
+        for k in range(begin, end):
             high, low = split(charged * wy[number, k : k + 1])
-            column_hi[k * size_x : (k + 1) * size_x] = high
-            column_lo[k * size_x : (k + 1) * size_x] = low
+            at = (k - begin) * size_x
+            column_hi[at : at + size_x] = high
+            column_lo[at : at + size_x] = low
         lanes = pl.ds(2 * number * SLOTS, SLOTS)
-        total = size_x * size_y
+        total = size_x * (end - begin)
         return product((column_hi[:total], column_lo[:total]), (wz_hi[:, lanes], wz_lo[:, lanes]), NT)
 
-    side_tables(0)
-    depth_tables(0, 0)
-
-    pl.semaphore_wait(barrier, COUNT - 1)
+    pl.semaphore_wait(barrier, N_PX + N_PY)
 
     atom_copies = []
     for number in range(1, 4):
@@ -325,86 +352,161 @@
         copy.start()
         atom_copies.append(copy)
 
-    grid[:CELLS] = spread(0)
-    grid[CELLS:] = jnp.zeros((CHUNKS * HALF + HALF - CELLS, GRID), jnp.float32)
+    def vouch(step, carry):
+        pl.semaphore_signal(vouched, inc=1, device_id=(lax.rem(px + step, N_PX), py), device_id_type=MESH)
+        return carry
+
+    lax.fori_loop(1, N_PX, vouch, 0)
+
+    side_tables(0)
+    depth_tables(0)
+
+    def spread_near(number, begin, end):
+        size_x = CLASSES[number][2]
+        added = spread(number, begin, end)
+        for k in range(begin, min(end, CLASSES[number][3])):
+            at = (k - begin) * size_x
+            grid[k * WIDE_X : k * WIDE_X + size_x] += added[at : at + size_x]
+
+    def transform(begin, end):
+        lanes = end - begin + (end - begin) % 2
+        dense = split(grid[begin * HALF : (begin + lanes) * HALF])
+        cosine_part = product((line_hi[:ROWS], line_lo[:ROWS]), dense, NT)
+        sine_part = product((line_hi[PADDED : PADDED + ROWS], line_lo[PADDED : PADDED + ROWS]), dense, NT)
+        lower = lax.broadcasted_iota(jnp.int32, (ROWS, LANES), 1) < HALF
+        for j in range(begin, end):
+            at = ((j - begin) // 2) * LANES
+            cosine_block = cosine_part[:, at : at + LANES]
+            sine_block = sine_part[:, at : at + LANES]
+            if (j - begin) % 2 == 0:
+                outbound[j] = jnp.where(lower, cosine_block, swap(sine_block))
+            else:
+                outbound[j] = jnp.where(lower, swap(cosine_block), sine_block)
+
+    first, second = GROUPS
+    grid[: second[2] * WIDE_X] = spread(0, *first[2:])
+    grid[CELLS:] = jnp.zeros((HALF, GRID), jnp.float32)
     for number in range(1, 4):
         atom_copies[number - 1].wait_recv()
         side_tables(number)
-        depth_tables(number, 0)
-        size_x, size_y = CLASSES[number][2:]
-        added = spread(number)
-        for k in range(size_y):
-            grid[k * WIDE_X : k * WIDE_X + size_x] += added[k * size_x : (k + 1) * size_x]
-
+        depth_tables(number)
+        spread_near(number, *first[2:])
     tables[0].wait()
     tables[1].wait()
-    dense = split(grid[...])
-    cosine_part = product((line_hi[:ROWS], line_lo[:ROWS]), dense, NT)
-    sine_part = product((line_hi[PADDED : PADDED + ROWS], line_lo[PADDED : PADDED + ROWS]), dense, NT)
-    lower = lax.broadcasted_iota(jnp.int32, (ROWS, LANES), 1) < HALF
-    for j in range(CHUNKS):
-        at = (j // 2) * LANES
-        cosine_block = cosine_part[:, at : at + LANES]
-        sine_block = sine_part[:, at : at + LANES]
-        if j % 2 == 0:
-            outbound[j] = jnp.where(lower, cosine_block, swap(sine_block))
-        else:
-            outbound[j] = jnp.where(lower, swap(cosine_block), sine_block)
-
-    def send_line(line, to_x, to_y):
-        mine = jnp.logical_and(to_x == px, to_y == py)
-
-        @pl.when(mine)
-        def _():
-            pltpu.make_async_copy(outbound.at[:, pl.ds(line, 1), :], inbound.at[:, pl.ds(me, 1), :], out_recv).start()
-
-        @pl.when(jnp.logical_not(mine))
-        def _():
-            pltpu.make_async_remote_copy(
-                outbound.at[:, pl.ds(line, 1), :],
-                inbound.at[:, pl.ds(me, 1), :],
-                out_send,
-                out_recv,
-                device_id=(to_x, to_y),
-                device_id_type=MESH,
-            ).start()
-
-    def send_even(step, carry):
-        line = lax.rem(step + me, 128)
-        send_line(line, 2 * (line // N_PY), lax.rem(line, N_PY))
-        return carry
-
-    def send_odd(step, carry):
-        line = lax.rem(step + me, 64)
-        depth = line // 16
-        pair = 2 * lax.rem(line, 16)
-        send_line(128 + line, 2 * depth + 1, pair + lax.rem(depth + pair // 4, 2))
-        return carry
-
-    lax.fori_loop(0, 128, send_even, 0)
-    lax.fori_loop(0, 64, send_odd, 0)
-    send_line(LINES - 1, 1, 1)
-
-    odd = lax.rem(px, 2)
-    depth = px // 2
-    order = depth * N_PY + py
+    transform(*first[:2])
+    pl.semaphore_wait(vouched, N_PX - 1)
+
+    core_me = lax.rem(px, 2)
+    low_me = lax.div(px, 2)
+    x_me = lax.rem(lax.div(py, 4), 4)
+    y_me = lax.rem(py, 4)
+
+    order = low_me * N_PY + py
     last = jnp.logical_and(px == 1, py == 1)
-    matching = lax.rem(depth + py // 4 + py, 2) == 0
-    active = jnp.logical_or(jnp.logical_or(odd == 0, last), matching)
-    line_me = (1 - odd) * order + odd * (128 + order // 2)
+    matching = jnp.logical_and(core_me == 1, lax.rem(low_me + x_me + y_me, 2) == 0)
+    active = jnp.logical_or(jnp.logical_or(core_me == 0, last), matching)
+    line_me = (1 - core_me) * order + core_me * (128 + lax.div(order, 2))
     line_me = line_me + last.astype(jnp.int32) * (LINES - 1 - 128)
 
-    for number in range(4):
-        depth_tables(number, 1)
+    def part(buffer, group, row):
+        begin, end = GROUPS[group][:2]
+        return buffer.at[pl.ds(begin, end - begin), pl.ds(row, 1), :]
+
+    def keep_line(group):
+        pltpu.make_async_copy(part(outbound, group, line_me), part(inbound, group, me), out_recv.at[group]).start()
+
+    def send_line(group, line, to_x, to_y):
+        pltpu.make_async_remote_copy(
+            part(outbound, group, line),
+            part(inbound, group, me),
+            out_send.at[group],
+            out_recv.at[group],
+            device_id=(to_x, to_y),
+            device_id_type=MESH,
+        ).start()
+
+    def send_even(group, step):
+        line = lax.rem(order + step, 128)
+        send_line(group, line, 2 * lax.div(line, N_PY), lax.rem(line, N_PY))
+
+    def send_odd(group, step):
+        pair = lax.rem(lax.div(order, 2) + step, 64)
+        low = lax.div(pair, 16)
+        to_y = 2 * lax.rem(pair, 16)
+        send_line(group, 128 + pair, 2 * low + 1, to_y + lax.rem(low + lax.div(to_y, 4), 2))
+
+    def send_group(group):
+        pl.when(active)(lambda: keep_line(group))
+        pl.when(core_me == 1)(lambda: send_even(group, 0))
+        pl.when(jnp.logical_not(matching))(lambda: send_odd(group, 0))
+        pl.when(jnp.logical_not(last))(lambda: send_line(group, LINES - 1, 1, 1))
+        send_even(group, 1)
+
+        def send_evens(step, carry):
+            for k in range(7):
+                send_even(group, 2 + 7 * step + k)
+            slope_block(27 * group + step)
+            return carry
+
+        def send_odds(step, carry):
+            for k in range(7):
+                send_odd(group, 1 + 7 * step + k)
+            slope_block(27 * group + 18 + step)
+            return carry
+
+        lax.fori_loop(0, 18, send_evens, 0)
+        lax.fori_loop(0, 9, send_odds, 0)
+
+    send_group(0)
+    grid[second[2] * WIDE_X : CELLS] = spread(0, *second[2:])
+    spread_near(2, *second[2:])
+    transform(*second[:2])
+    send_group(1)
+
     for table in tables[2:]:
         table.wait()
 
-    def wait_rows(buffer, count, semaphore):
-        view = buffer.at[:, pl.ds(0, count), :]
-        pltpu.make_async_copy(view, view, semaphore).wait()
+    def wait_rows(buffer, group, count, semaphores):
+        begin, end = GROUPS[group][:2]
+        view = buffer.at[pl.ds(begin, end - begin), pl.ds(0, count), :]
+        pltpu.make_async_copy(view, view, semaphores.at[group]).wait()
 
     @pl.when(active)
     def _():
+        left = lax.broadcasted_iota(jnp.int32, (COUNT, LANES), 1) < HALF
+        brick_pair = (brick_hi[...], brick_lo[...])
+
+        def pairs(group):
+            begin, end = GROUPS[group][:2]
+            return [(j, min(j + 2, end)) for j in range(begin, end, 2)]
+
+        def turned(value, j):
+            return value * twiddle[0, j] + swap(value) * twiddle[1, j]
+
+        def gather(group):
+            for begin, end in pairs(group):
+                block = jnp.concatenate([inbound[j] for j in range(begin, end)], axis=1)
+                mixed = product(brick_pair, split(block), NN)
+                for j in range(begin, end):
+                    at = (j - begin) * LANES
+                    upper = mixed[:COUNT, at : at + LANES]
+                    crossed = swap(mixed[COUNT:, at : at + LANES])
+                    value = upper + jnp.where(left, -crossed, crossed)
+                    high, low = split(turned(value, j))
+                    first_hi[:, j * LANES : (j + 1) * LANES] = high
+                    first_lo[:, j * LANES : (j + 1) * LANES] = low
+
+        def over_cells(group, lanes):
+            rows = slice(GROUPS[group][0] * LANES, GROUPS[group][1] * LANES)
+            return product((first_hi[:, rows], first_lo[:, rows]), (cell_hi[rows, lanes], cell_lo[rows, lanes]), NN)
+
+        every = pairs(0) + pairs(1)
+        wait_rows(inbound, 0, COUNT, out_recv)
+        gather(0)
+        for begin, end in every:
+            lanes = slice(begin * LANES, end * LANES)
+            spectrum[:, lanes] = over_cells(0, lanes)
+
         scalars = line_green[pl.ds(line_me, 1), :]
         square_z = scalars[:, :LANES]
         gain_z = scalars[:, LANES:]
@@ -414,82 +516,75 @@
             bounded = jnp.where(positive, squared, 1.0)
             multiplier[j] = jnp.where(positive, green[1, j] * gain_z / bounded, 0.0)
 
-        wait_rows(inbound, COUNT, out_recv)
-        left = lax.broadcasted_iota(jnp.int32, (COUNT, LANES), 1) < HALF
-        groups = [(0, 2), (2, 4), (4, 6), (6, 8), (8, 9)]
-        brick_pair = (brick_hi[...], brick_lo[...])
-
-        def turned(value, j):
-            return value * twiddle[0, j] + swap(value) * twiddle[1, j]
-
-        for begin, end in groups:
-            block = jnp.concatenate([inbound[j] for j in range(begin, end)], axis=1)
-            mixed = product(brick_pair, split(block), NN)
-            for j in range(begin, end):
-                at = (j - begin) * LANES
-                upper = mixed[:COUNT, at : at + LANES]
-                crossed = swap(mixed[COUNT:, at : at + LANES])
-                value = upper + jnp.where(left, -crossed, crossed)
-                high, low = split(turned(value, j))
-                first_hi[:, j * LANES : (j + 1) * LANES] = high
-                first_lo[:, j * LANES : (j + 1) * LANES] = low
-        for begin, end in groups:
+        wait_rows(inbound, 1, COUNT, out_recv)
+        gather(1)
+        for begin, end in every:
             lanes = slice(begin * LANES, end * LANES)
-            block = product((first_hi[...], first_lo[...]), (cell_hi[:, lanes], cell_lo[:, lanes]), NN)
+            block = spectrum[:, lanes] + over_cells(1, lanes)
             for j in range(begin, end):
                 at = (j - begin) * LANES
                 high, low = split(block[:, at : at + LANES] * multiplier[j])
                 second_hi[:, j * LANES : (j + 1) * LANES] = high
                 second_lo[:, j * LANES : (j + 1) * LANES] = low
-        for begin, end in groups:
-            lanes = slice(begin * LANES, end * LANES)
-            block = product((second_hi[...], second_lo[...]), (cell_hi[:, lanes], cell_lo[:, lanes]), NN)
-            block = jnp.concatenate(
-                [turned(block[:, (j - begin) * LANES : (j - begin + 1) * LANES], j) for j in range(begin, end)], axis=1
-            )
-            mixed = product(brick_pair, split(block), NN)
-            for j in range(begin, end):
-                at = (j - begin) * LANES
-                upper = mixed[:COUNT, at : at + LANES]
-                crossed = swap(mixed[COUNT:, at : at + LANES])
-                returning[j] = jnp.where(left, upper, -upper) - crossed
-
-        def send_back(step, carry):
-            other = lax.rem(me + step, COUNT)
+
+        def send_row(group, other):
             pltpu.make_async_remote_copy(
-                returning.at[:, pl.ds(other, 1), :],
-                returned.at[:, pl.ds(line_me, 1), :],
-                back_send,
-                back_recv,
-                device_id=(other // N_PY, lax.rem(other, N_PY)),
+                part(returning, group, other),
+                part(returned, group, line_me),
+                back_send.at[group],
+                back_recv.at[group],
+                device_id=(lax.div(other, N_PY), lax.rem(other, N_PY)),
                 device_id_type=MESH,
             ).start()
-            return carry
-
-        pltpu.make_async_copy(returning.at[:, pl.ds(me, 1), :], returned.at[:, pl.ds(line_me, 1), :], back_recv).start()
-        lax.fori_loop(1, COUNT, send_back, 0)
-
-    wait_rows(returned, LINES, back_recv)
-    for j in range(CHUNKS):
-        high, low = split(returned[j].T)
-        rows = slice(j * HALF, (j + 1) * HALF)
-        turned_hi[rows, :PADDED] = high[:HALF]
-        turned_hi[rows, PADDED:] = high[HALF:]
-        turned_lo[rows, :PADDED] = low[:HALF]
-        turned_lo[rows, PADDED:] = low[HALF:]
-    high, low = split(product((turned_hi[...], turned_lo[...]), (line_hi[...], line_lo[...]), NN))
-    field_hi[...] = high
-    field_lo[...] = low
-
-    def sample(number):
-        size_x, size_y = CLASSES[number][2:]
-        total = size_x * size_y
+
+        for group in range(2):
+            for begin, end in pairs(group):
+                lanes = slice(begin * LANES, end * LANES)
+                block = product((second_hi[...], second_lo[...]), (cell_hi[:, lanes], cell_lo[:, lanes]), NN)
+                block = jnp.concatenate(
+                    [turned(block[:, (j - begin) * LANES : (j - begin + 1) * LANES], j) for j in range(begin, end)], axis=1
+                )
+                mixed = product(brick_pair, split(block), NN)
+                for j in range(begin, end):
+                    at = (j - begin) * LANES
+                    upper = mixed[:COUNT, at : at + LANES]
+                    crossed = swap(mixed[COUNT:, at : at + LANES])
+                    returning[j] = jnp.where(left, upper, -upper) - crossed
+
+            def send_back(step, carry, group=group):
+                for k in range(5):
+                    send_row(group, lax.rem(me + 1 + 5 * step + k, COUNT))
+                return carry
+
+            pltpu.make_async_copy(part(returning, group, me), part(returned, group, line_me), back_recv.at[group]).start()
+            lax.fori_loop(0, (COUNT - 1) // 5, send_back, 0)
+
+    def restore(group):
+        begin, end = GROUPS[group][:2]
+        wait_rows(returned, group, LINES, back_recv)
+        for j in range(begin, end):
+            high, low = split(returned[j].T)
+            rows = slice(j * HALF, (j + 1) * HALF)
+            turned_hi[rows, :PADDED] = high[:HALF]
+            turned_hi[rows, PADDED:] = high[HALF:]
+            turned_lo[rows, :PADDED] = low[:HALF]
+            turned_lo[rows, PADDED:] = low[HALF:]
+        rows = slice(begin * HALF, end * HALF)
+        high, low = split(product((turned_hi[rows], turned_lo[rows]), (line_hi[...], line_lo[...]), NN))
+        field_hi[rows] = high
+        field_lo[rows] = low
+
+    def sample(number, begin, end):
+        size_x = CLASSES[number][2]
+        end = min(end, CLASSES[number][3])
+        total = size_x * (end - begin)
         if size_x == WIDE_X:
-            field = (field_hi[:total], field_lo[:total])
+            rows = slice(begin * WIDE_X, end * WIDE_X)
+            field = (field_hi[rows], field_lo[rows])
         else:
             field = tuple(
-                jnp.concatenate([part[k * WIDE_X : k * WIDE_X + size_x] for k in range(size_y)], axis=0)
-                for part in (field_hi, field_lo)
+                jnp.concatenate([values[k * WIDE_X : k * WIDE_X + size_x] for k in range(begin, end)], axis=0)
+                for values in (field_hi, field_lo)
             )
         lanes = slice(2 * number * SLOTS, 2 * (number + 1) * SLOTS)
         sampled[:total] = product(field, (wz_hi[:, lanes], wz_lo[:, lanes]), NN)
@@ -500,8 +595,8 @@
             over_y = jnp.zeros((size_x, LANES), jnp.float32)
             slope_over_y = over_y
             rising_over_y = over_y
-            for k in range(size_y):
-                rows = slice(k * size_x, (k + 1) * size_x)
+            for k in range(begin, end):
+                rows = slice((k - begin) * size_x, (k - begin + 1) * size_x)
                 level = sampled[rows, here]
                 rising = sampled[rows, pl.ds(SLOTS + at, LANES)]
                 weight = wy[number, k : k + 1, here]
@@ -509,17 +604,19 @@
                 slope_over_y += sy[number, k : k + 1, here] * level
                 rising_over_y += weight * rising
             weight = wx[number, :size_x, here]
-            partials[number, 0:1, here] = jnp.sum(weight * over_y, axis=0, keepdims=True)
-            partials[number, 1:2, here] = jnp.sum(sx[number, :size_x, here] * over_y, axis=0, keepdims=True)
-            partials[number, 2:3, here] = jnp.sum(weight * slope_over_y, axis=0, keepdims=True)
-            partials[number, 3:4, here] = jnp.sum(weight * rising_over_y, axis=0, keepdims=True)
+            sums = [weight * over_y, sx[number, :size_x, here] * over_y, weight * slope_over_y, weight * rising_over_y]
+            for row, values in enumerate(sums):
+                total_row = jnp.sum(values, axis=0, keepdims=True)
+                if begin > 0:
+                    total_row = total_row + partials[number, row : row + 1, here]
+                partials[number, row : row + 1, here] = total_row
             return carry
 
         lax.fori_loop(0, SLOTS // LANES, block, 0)
 
     part_copies = []
-    for number in range(1, 4):
-        sample(number)
+
+    def give(number):
         step_x, step_y = CLASSES[number][:2]
         target = (lax.rem(px + N_PX - step_x, N_PX), lax.rem(py + N_PY - step_y, N_PY))
         copy = pltpu.make_async_remote_copy(
@@ -532,26 +629,39 @@
         )
         copy.start()
         part_copies.append(copy)
-    sample(0)
+
+    restore(0)
+    for number in (1, 3):
+        sample(number, *first[2:])
+        give(number)
+    sample(2, *first[2:])
+    sample(0, *first[2:])
+    restore(1)
+    sample(2, *second[2:])
+    give(2)
+    sample(0, *second[2:])
     summed = partials[0, 0:4]
+    for copy in part_copies:
+        copy.wait_recv()
     for number in range(1, 4):
-        part_copies[number - 1].wait_recv()
         summed = summed + received[number, 0:4]
-    potential_out[0] = summed[0:1] * occupied
+    result[0, 0] = summed[0:1] * occupied
     for d in range(3):
-        force_out[d, 0] = -weighted * summed[1 + d : 2 + d]
+        result[1 + d, 0] = -weighted * summed[1 + d : 2 + d]
 
     for copy in atom_copies + part_copies:
         copy.wait_send()
 
     @pl.when(active)
     def _():
-        wait_rows(outbound, LINES - 1, out_send)
-        wait_rows(returning, COUNT - 1, back_send)
+        for group in range(2):
+            wait_rows(outbound, group, LINES - 1, out_send)
+            wait_rows(returning, group, COUNT - 1, back_send)
 
     @pl.when(jnp.logical_not(active))
     def _():
-        wait_rows(outbound, LINES, out_send)
+        for group in range(2):
+            wait_rows(outbound, group, LINES, out_send)
 
 
 def shards(charges, cells, fractions, filled):
@@ -568,11 +678,11 @@
     plane = vmem((COUNT, 2 * CELLS), bf16)
     whole = pl.BlockSpec(memory_space=pltpu.VMEM)
     distant = pl.BlockSpec(memory_space=pl.ANY)
-    return pl.pallas_call(
+    result = pl.pallas_call(
         kernel,
-        out_shape=(jax.ShapeDtypeStruct((1, 1, SLOTS), f32), jax.ShapeDtypeStruct((3, 1, 1, SLOTS), f32)),
+        out_shape=jax.ShapeDtypeStruct((4, 1, 1, SLOTS), f32),
         in_specs=[whole] * 4 + [distant] * 8 + [whole],
-        out_specs=(whole, whole),
+        out_specs=whole,
         scratch_shapes=[
             vmem((2 * PADDED, GRID), bf16),
             vmem((2 * PADDED, GRID), bf16),
@@ -605,23 +715,27 @@
             vmem((CELLS, 2 * PADDED), bf16),
             vmem((CELLS, GRID), bf16),
             vmem((CELLS, GRID), bf16),
+            vmem((COUNT, 2 * CELLS), f32),
+            vmem((4, 8, SLOTS), f32),
             vmem((CELLS, 2 * SLOTS), f32),
             vmem((4, 8, SLOTS), f32),
             vmem((4, 8, SLOTS), f32),
             pltpu.SemaphoreType.DMA((8,)),
             pltpu.SemaphoreType.DMA((4,)),
             pltpu.SemaphoreType.DMA((4,)),
-            pltpu.SemaphoreType.DMA,
-            pltpu.SemaphoreType.DMA,
-            pltpu.SemaphoreType.DMA,
-            pltpu.SemaphoreType.DMA,
+            pltpu.SemaphoreType.DMA((2,)),
+            pltpu.SemaphoreType.DMA((2,)),
+            pltpu.SemaphoreType.DMA((2,)),
+            pltpu.SemaphoreType.DMA((2,)),
             pltpu.SemaphoreType.DMA((4,)),
             pltpu.SemaphoreType.DMA((4,)),
+            pltpu.SemaphoreType.REGULAR,
         ],
         compiler_params=pltpu.CompilerParams(
             collective_id=0, has_side_effects=True, vmem_limit_bytes=56 * 1024 * 1024
         ),
     )(charges, cells, fractions, filled, *[jnp.asarray(table) for table in constants])
+    return result[0], result[1:]
 
 
 def solution(mesh):

time: 102 us -> 89.7 us (0.88)
  the two profiles are of different devices: /device:TPU:63 before, /device:TPU:1 now
where the time goes in v2:
time: 89.7 us; the launch traced here: 89.5 us
  Pallas kernels  85.7 us (96%)
  local copies, waits for them, and re-layouts  2.55 us (3%)
  between operations  1.29 us (1%)
    pallas_call x1, Pallas kernels, shards(): pl.pallas_call(kernel, out_shape=jax.ShapeDtypeStruct((4, 1, 1, SLOTS), f...  85.7 us

profile of v2, /device:TPU:1, one launch (start us, length us, event | category | flops | bytes accessed | tf_op | source)
XLA Modules:
  0.0 89.5 jit_solution(5183412618508118514)
XLA Ops:
  1.3 85.7 %shard_map.140 = f32[4,1,1,512]{3,2,1,0:T(1,128)} custom-call(f32[1,1,512]{2,1,0:T(1,128)} %charges.1, s32[3,1,1,512]{3,2,1,0:T(1,128)} %cells.1, f32[3,1,1,512]{3,2,1,0:T(1,128)} %fractions.1, s32[1,1]{1,0:T(1,128)S(6)} %copy.15.filled, bf16[512,384]{1,0:T(8,128)(2,1)} %constant.18.clone.line_hi_any, bf16[512,384]{1,0:T(8,128)(2,1)} %constant.19.clone.line_lo_any, ...), custom_call_target="tpu_custom_call" | custom-call | tf_op jit(solution)/shard_map/pallas_call | solution.py:681
  87.0 1.3 %slice_bitcast_fusion = f32[1,1,512]{2,1,0:T(1,128)} fusion(f32[4,1,1,512]{3,2,1,0:T(1,128)} %shard_map.140), kind=kLoop, calls=%fused_computation | loop fusion | bytes 4096 | tf_op jit(solution)/shard_map/squeeze | solution.py:738
  88.2 1.3 %slice.7 = f32[3,1,1,512]{3,2,1,0:T(1,128)} slice(f32[4,1,1,512]{3,2,1,0:T(1,128)} %shard_map.140), slice={[1:4], [0:1], [0:1], [0:512]} | slice | bytes 12288 | tf_op jit(solution)/shard_map/slice | solution.py:738

commit v3 on v2

--- a/solution.py
+++ b/solution.py
@@ -31,7 +31,15 @@
 MESH = pl.DeviceIdType.MESH
 NT = (((1,), (1,)), ((), ()))
 NN = (((1,), (0,)), ((), ()))
-GROUPS = ((0, 6, 0, 8), (6, 9, 8, 12))
+GROUPS = ((0, 6), (6, 9))
+FULL_Y = 6
+RUNS = (
+    [((y, 0, WIDE_X), y * WIDE_X) for y in range(FULL_Y)]
+    + [((y, 0, EDGE_X), FULL_Y * WIDE_X + (y - FULL_Y) * EDGE_X) for y in range(FULL_Y, WIDE_Y)]
+    + [((y, EDGE_X, WIDE_X), 2 * CELLS // 3 + (y - FULL_Y) * (WIDE_X - EDGE_X)) for y in range(FULL_Y, WIDE_Y)]
+)
+CELL_Y = np.concatenate([np.full(end - begin, y) for (y, begin, end), _ in RUNS])
+CELL_X = np.concatenate([np.arange(begin, end) for (_, begin, end), _ in RUNS])
 CLASSES = ((0, 0, WIDE_X, WIDE_Y), (0, 1, WIDE_X, EDGE_Y), (1, 0, EDGE_X, WIDE_Y), (1, 1, EDGE_X, EDGE_Y))
 
 
@@ -69,17 +77,15 @@
 
 def twiddle_tables():
     device = np.arange(COUNT)
-    cell = np.arange(CELLS)
     a, b = device // N_PY, device % N_PY
-    y, x = cell // WIDE_X, cell % WIDE_X
+    y, x = CELL_Y, CELL_X
     angles = turn(a[:, None] * x[None, :] + b[:, None] * y[None, :], GRID)
     cosines, sines = np.cos(angles), -np.sin(angles)
     return chunked(cosines, cosines), chunked(-sines, sines)
 
 
 def cell_table():
-    cell = np.arange(CELLS)
-    y, x = cell // WIDE_X, cell % WIDE_X
+    y, x = CELL_Y, CELL_X
     angles = turn(4 * y[:, None] * y[None, :] + x[:, None] * x[None, :], WIDE_X)
     cosines, sines = np.cos(angles), -np.sin(angles)
     table = np.zeros((CHUNKS, 2, HALF, CHUNKS, 2, HALF))
@@ -105,9 +111,8 @@
 
 def green_tables():
     device = np.arange(COUNT)
-    cell = np.arange(CELLS)
-    freq_x = (device // N_PY)[:, None] + N_PX * (cell % WIDE_X)[None, :]
-    freq_y = (device % N_PY)[:, None] + N_PY * (cell // WIDE_X)[None, :]
+    freq_x = (device // N_PY)[:, None] + N_PX * CELL_X[None, :]
+    freq_y = (device % N_PY)[:, None] + N_PY * CELL_Y[None, :]
     square_x, modulus_x = axis_terms(freq_x)
     square_y, modulus_y = axis_terms(freq_y)
     squares = square_x + square_y
@@ -169,14 +174,28 @@
     return total
 
 
+def runs_of(number, second):
+    size_x, size_y = CLASSES[number][2:]
+    found = []
+    for (y, begin, end), at in RUNS:
+        if (at >= 2 * CELLS // 3) == second and y < size_y and begin < size_x:
+            found.append((y, begin, min(end, size_x), at))
+    return found
+
+
 def swap(value):
     return pltpu.roll(value, HALF, 1)
 
 
+def hand_over(result, potentials, forces):
+    potentials[...] = result[0]
+    forces[...] = result[1:4]
+
+
 def kernel(
-    charges,
-    cells,
-    fractions,
+    charges_any,
+    cells_any,
+    fractions_any,
     filled,
     line_hi_any,
     line_lo_any,
@@ -186,8 +205,12 @@
     cell_lo_any,
     twiddle_any,
     green_any,
+    line_green_any,
+    result,
+    charges,
+    cells,
+    fractions,
     line_green,
-    result,
     line_hi,
     line_lo,
     brick_hi,
@@ -220,7 +243,9 @@
     field_hi,
     field_lo,
     spectrum,
-    rises_z,
+    taps_hi,
+    taps_lo,
+    offsets,
     sampled,
     partials,
     received,
@@ -239,6 +264,15 @@
     py = lax.axis_index("py")
     me = px * N_PY + py
 
+    arguments = [
+        pltpu.make_async_copy(source, target, table_sems.at[9 + number])
+        for number, (source, target) in enumerate(
+            [(charges_any, charges), (cells_any, cells), (fractions_any, fractions)]
+        )
+    ]
+    for copy in arguments:
+        copy.start()
+
     barrier = pltpu.get_barrier_semaphore()
 
     def greet(target):
@@ -269,11 +303,14 @@
                 (green_any, green),
                 (cell_hi_any, cell_hi),
                 (cell_lo_any, cell_lo),
+                (line_green_any, line_green),
             ]
         )
     ]
     for table in tables:
         table.start()
+    for copy in arguments:
+        copy.wait()
 
     slot = lax.broadcasted_iota(jnp.int32, (1, SLOTS), 1)
     occupied = (slot < filled[...]).astype(jnp.float32)
@@ -288,6 +325,7 @@
     def side_tables(number):
         step_x, step_y, size_x, size_y = CLASSES[number]
         values, slopes = spline_rows(atoms[number, 4:7])
+        depth_rows(number, values, slopes)
         for row, step, wide, size, weights, rises in (
             (0, step_x, WIDE_X, size_x, wx, sx),
             (1, step_y, WIDE_Y, 16, wy, sy),
@@ -297,22 +335,30 @@
             weights[number, :size] = place(offset, [v[row : row + 1] for v in values])
             rises[number, :size] = place(offset, [v[row : row + 1] for v in slopes])
 
-    def depth_block(start, rows, at, lanes):
-        offset = lax.broadcasted_iota(jnp.int32, (16, SLOTS), 0) + at - start
-        offset = jnp.where(offset < 0, offset + GRID, offset)
-        high, low = split(place(offset, rows))
+    def depth_rows(number, values, slopes):
+        for kind, rows in enumerate((values, slopes)):
+            for j in range(ORDER):
+                high, low = split(jnp.broadcast_to(rows[j][2:3], (16, SLOTS)))
+                taps_hi[number, kind, j] = high
+                taps_lo[number, kind, j] = low
+        start = atoms[number, 3:4].astype(jnp.int32)
+        offsets[number] = (lax.broadcasted_iota(jnp.int32, (16, SLOTS), 0) - start).astype(jnp.int16)
+
+    def depth_block(number, kind, at, lanes):
+        offset = offsets[number] + jnp.full((16, SLOTS), at, jnp.int32).astype(jnp.int16)
+        offset = jnp.where(offset < 0, offset + jnp.int16(GRID), offset)
+        high = jnp.zeros((16, SLOTS), jnp.bfloat16)
+        low = high
+        for j in range(ORDER):
+            here = offset == j
+            high = jnp.where(here, taps_hi[number, kind, j], high)
+            low = jnp.where(here, taps_lo[number, kind, j], low)
         wz_hi[pl.ds(at, 16), lanes] = high
         wz_lo[pl.ds(at, 16), lanes] = low
 
     def depth_tables(number):
-        values, slopes = spline_rows(atoms[number, 4:7])
-        rows = [v[2:3] for v in values]
-        start = atoms[number, 3:4].astype(jnp.int32)
-        for j in range(ORDER):
-            rises_z[number, j : j + 1] = slopes[j][2:3]
-
         def block(step, carry):
-            depth_block(start, rows, pl.multiple_of(step * 16, 16), pl.ds(2 * number * SLOTS, SLOTS))
+            depth_block(number, 0, pl.multiple_of(step * 16, 16), pl.ds(2 * number * SLOTS, SLOTS))
             return carry
 
         lax.fori_loop(0, GRID // 16, block, 0)
@@ -321,23 +367,19 @@
         step = jnp.minimum(step, 4 * GRID // 32 - 1)
         number = lax.div(step, GRID // 32)
         at = lax.rem(step, GRID // 32) * 32
-        rows = [rises_z[number, j : j + 1] for j in range(ORDER)]
-        start = atoms[number, 3:4].astype(jnp.int32)
         lanes = pl.ds(pl.multiple_of((2 * number + 1) * SLOTS, SLOTS), SLOTS)
         for k in range(2):
-            depth_block(start, rows, pl.multiple_of(at + 16 * k, 16), lanes)
-
-    def spread(number, begin, end):
-        size_x = CLASSES[number][2]
-        end = min(end, CLASSES[number][3])
-        charged = wx[number, :size_x] * atoms[number, 0:1]
-        for k in range(begin, end):
-            high, low = split(charged * wy[number, k : k + 1])
-            at = (k - begin) * size_x
-            column_hi[at : at + size_x] = high
-            column_lo[at : at + size_x] = low
+            depth_block(number, 1, pl.multiple_of(at + 16 * k, 16), lanes)
+
+    def spread(number, second):
+        charge = atoms[number, 0:1]
+        total = 0
+        for y, begin, end, _ in runs_of(number, second):
+            high, low = split((wx[number, begin:end] * charge) * wy[number, y : y + 1])
+            column_hi[total : total + end - begin] = high
+            column_lo[total : total + end - begin] = low
+            total += end - begin
         lanes = pl.ds(2 * number * SLOTS, SLOTS)
-        total = size_x * (end - begin)
         return product((column_hi[:total], column_lo[:total]), (wz_hi[:, lanes], wz_lo[:, lanes]), NT)
 
     pl.semaphore_wait(barrier, N_PX + N_PY)
@@ -361,12 +403,12 @@
     side_tables(0)
     depth_tables(0)
 
-    def spread_near(number, begin, end):
-        size_x = CLASSES[number][2]
-        added = spread(number, begin, end)
-        for k in range(begin, min(end, CLASSES[number][3])):
-            at = (k - begin) * size_x
-            grid[k * WIDE_X : k * WIDE_X + size_x] += added[at : at + size_x]
+    def spread_near(number):
+        added = spread(number, False)
+        place_at = 0
+        for _, begin, end, at in runs_of(number, False):
+            grid[at : at + end - begin] += added[place_at : place_at + end - begin]
+            place_at += end - begin
 
     def transform(begin, end):
         lanes = end - begin + (end - begin) % 2
@@ -384,16 +426,16 @@
                 outbound[j] = jnp.where(lower, swap(cosine_block), sine_block)
 
     first, second = GROUPS
-    grid[: second[2] * WIDE_X] = spread(0, *first[2:])
+    grid[: first[1] * HALF] = spread(0, False)
     grid[CELLS:] = jnp.zeros((HALF, GRID), jnp.float32)
     for number in range(1, 4):
         atom_copies[number - 1].wait_recv()
         side_tables(number)
         depth_tables(number)
-        spread_near(number, *first[2:])
+        spread_near(number)
     tables[0].wait()
     tables[1].wait()
-    transform(*first[:2])
+    transform(*first)
     pl.semaphore_wait(vouched, N_PX - 1)
 
     core_me = lax.rem(px, 2)
@@ -401,11 +443,16 @@
     x_me = lax.rem(lax.div(py, 4), 4)
     y_me = lax.rem(py, 4)
 
+    def main_core(low, to_y):
+        return lax.rem(low + lax.div(to_y, 8) + lax.div(lax.rem(to_y, 4), 2), 2)
+
     order = low_me * N_PY + py
+    main_me = main_core(low_me, py)
+    other_me = lax.rem(core_me + main_me, 2)
     last = jnp.logical_and(px == 1, py == 1)
-    matching = jnp.logical_and(core_me == 1, lax.rem(low_me + x_me + y_me, 2) == 0)
-    active = jnp.logical_or(jnp.logical_or(core_me == 0, last), matching)
-    line_me = (1 - core_me) * order + core_me * (128 + lax.div(order, 2))
+    matching = jnp.logical_and(other_me == 1, lax.rem(low_me + x_me + y_me, 2) == 0)
+    active = jnp.logical_or(jnp.logical_or(other_me == 0, last), matching)
+    line_me = (1 - other_me) * order + other_me * (128 + lax.div(order, 2))
     line_me = line_me + last.astype(jnp.int32) * (LINES - 1 - 128)
 
     def part(buffer, group, row):
@@ -427,17 +474,19 @@
 
     def send_even(group, step):
         line = lax.rem(order + step, 128)
-        send_line(group, line, 2 * lax.div(line, N_PY), lax.rem(line, N_PY))
+        low, to_y = lax.div(line, N_PY), lax.rem(line, N_PY)
+        send_line(group, line, 2 * low + main_core(low, to_y), to_y)
 
     def send_odd(group, step):
         pair = lax.rem(lax.div(order, 2) + step, 64)
         low = lax.div(pair, 16)
         to_y = 2 * lax.rem(pair, 16)
-        send_line(group, 128 + pair, 2 * low + 1, to_y + lax.rem(low + lax.div(to_y, 4), 2))
+        to_y = to_y + lax.rem(low + lax.div(to_y, 4), 2)
+        send_line(group, 128 + pair, 2 * low + 1 - main_core(low, to_y), to_y)
 
     def send_group(group):
         pl.when(active)(lambda: keep_line(group))
-        pl.when(core_me == 1)(lambda: send_even(group, 0))
+        pl.when(other_me == 1)(lambda: send_even(group, 0))
         pl.when(jnp.logical_not(matching))(lambda: send_odd(group, 0))
         pl.when(jnp.logical_not(last))(lambda: send_line(group, LINES - 1, 1, 1))
         send_even(group, 1)
@@ -458,9 +507,8 @@
         lax.fori_loop(0, 9, send_odds, 0)
 
     send_group(0)
-    grid[second[2] * WIDE_X : CELLS] = spread(0, *second[2:])
-    spread_near(2, *second[2:])
-    transform(*second[:2])
+    grid[second[0] * HALF : CELLS] = spread(0, True)
+    transform(*second)
     send_group(1)
 
     for table in tables[2:]:
@@ -574,16 +622,15 @@
         field_hi[rows] = high
         field_lo[rows] = low
 
-    def sample(number, begin, end):
-        size_x = CLASSES[number][2]
-        end = min(end, CLASSES[number][3])
-        total = size_x * (end - begin)
-        if size_x == WIDE_X:
-            rows = slice(begin * WIDE_X, end * WIDE_X)
-            field = (field_hi[rows], field_lo[rows])
+    def sample(number, second):
+        runs = runs_of(number, second)
+        total = sum(end - begin for _, begin, end, _ in runs)
+        if number < 2:
+            first_at = runs[0][3]
+            field = (field_hi[first_at : first_at + total], field_lo[first_at : first_at + total])
         else:
             field = tuple(
-                jnp.concatenate([values[k * WIDE_X : k * WIDE_X + size_x] for k in range(begin, end)], axis=0)
+                jnp.concatenate([values[at : at + end - begin] for _, begin, end, at in runs], axis=0)
                 for values in (field_hi, field_lo)
             )
         lanes = slice(2 * number * SLOTS, 2 * (number + 1) * SLOTS)
@@ -592,22 +639,26 @@
         def block(step, carry):
             at = pl.multiple_of(step * LANES, LANES)
             here = pl.ds(at, LANES)
-            over_y = jnp.zeros((size_x, LANES), jnp.float32)
-            slope_over_y = over_y
-            rising_over_y = over_y
-            for k in range(begin, end):
-                rows = slice((k - begin) * size_x, (k - begin + 1) * size_x)
+            found = {}
+            row_at = 0
+            for y, begin, end, _ in runs:
+                rows = slice(row_at, row_at + end - begin)
+                row_at += end - begin
                 level = sampled[rows, here]
                 rising = sampled[rows, pl.ds(SLOTS + at, LANES)]
-                weight = wy[number, k : k + 1, here]
-                over_y += weight * level
-                slope_over_y += sy[number, k : k + 1, here] * level
-                rising_over_y += weight * rising
-            weight = wx[number, :size_x, here]
-            sums = [weight * over_y, sx[number, :size_x, here] * over_y, weight * slope_over_y, weight * rising_over_y]
-            for row, values in enumerate(sums):
-                total_row = jnp.sum(values, axis=0, keepdims=True)
-                if begin > 0:
+                weight = wy[number, y : y + 1, here]
+                terms = [weight * level, sy[number, y : y + 1, here] * level, weight * rising]
+                before = found.get((begin, end))
+                found[begin, end] = terms if before is None else [a + b for a, b in zip(before, terms)]
+            sums = None
+            for (begin, end), (over_y, slope_over_y, rising_over_y) in found.items():
+                weight = wx[number, begin:end, here]
+                terms = [weight * over_y, sx[number, begin:end, here] * over_y]
+                terms += [weight * slope_over_y, weight * rising_over_y]
+                terms = [jnp.sum(values, axis=0, keepdims=True) for values in terms]
+                sums = terms if sums is None else [a + b for a, b in zip(sums, terms)]
+            for row, total_row in enumerate(sums):
+                if second:
                     total_row = total_row + partials[number, row : row + 1, here]
                 partials[number, row : row + 1, here] = total_row
             return carry
@@ -631,15 +682,12 @@
         part_copies.append(copy)
 
     restore(0)
-    for number in (1, 3):
-        sample(number, *first[2:])
+    for number in range(1, 4):
+        sample(number, False)
         give(number)
-    sample(2, *first[2:])
-    sample(0, *first[2:])
+    sample(0, False)
     restore(1)
-    sample(2, *second[2:])
-    give(2)
-    sample(0, *second[2:])
+    sample(0, True)
     summed = partials[0, 0:4]
     for copy in part_copies:
         copy.wait_recv()
@@ -681,9 +729,13 @@
     result = pl.pallas_call(
         kernel,
         out_shape=jax.ShapeDtypeStruct((4, 1, 1, SLOTS), f32),
-        in_specs=[whole] * 4 + [distant] * 8 + [whole],
+        in_specs=[distant] * 3 + [whole] + [distant] * 9,
         out_specs=whole,
         scratch_shapes=[
+            vmem((1, 1, SLOTS), f32),
+            vmem((3, 1, 1, SLOTS), jnp.int32),
+            vmem((3, 1, 1, SLOTS), f32),
+            vmem((ROWS, 2 * LANES), f32),
             vmem((2 * PADDED, GRID), bf16),
             vmem((2 * PADDED, GRID), bf16),
             vmem((2 * COUNT, COUNT), bf16),
@@ -716,11 +768,13 @@
             vmem((CELLS, GRID), bf16),
             vmem((CELLS, GRID), bf16),
             vmem((COUNT, 2 * CELLS), f32),
-            vmem((4, 8, SLOTS), f32),
+            vmem((4, 2, ORDER, 16, SLOTS), bf16),
+            vmem((4, 2, ORDER, 16, SLOTS), bf16),
+            vmem((4, 16, SLOTS), jnp.int16),
             vmem((CELLS, 2 * SLOTS), f32),
             vmem((4, 8, SLOTS), f32),
             vmem((4, 8, SLOTS), f32),
-            pltpu.SemaphoreType.DMA((8,)),
+            pltpu.SemaphoreType.DMA((12,)),
             pltpu.SemaphoreType.DMA((4,)),
             pltpu.SemaphoreType.DMA((4,)),
             pltpu.SemaphoreType.DMA((2,)),
@@ -735,7 +789,12 @@
             collective_id=0, has_side_effects=True, vmem_limit_bytes=56 * 1024 * 1024
         ),
     )(charges, cells, fractions, filled, *[jnp.asarray(table) for table in constants])
-    return result[0], result[1:]
+    return pl.pallas_call(
+        hand_over,
+        out_shape=(jax.ShapeDtypeStruct((1, 1, SLOTS), f32), jax.ShapeDtypeStruct((3, 1, 1, SLOTS), f32)),
+        in_specs=[whole],
+        out_specs=(whole, whole),
+    )(result)
 
 
 def solution(mesh):

time: 89.7 us -> 85.6 us (0.954)
  local copies, waits for them, and re-layouts: 2.55 us -> 0 us
  Pallas kernels: 85.7 us -> 84.2 us
    pallas_call x1, Pallas kernels: 85.7 us -> 82.9 us  [shards(): pl.pallas_call(kernel, out_shape=jax.ShapeDtypeStruct((4, 1, 1, SLOTS), f...]
    pallas_call x0 -> x1, Pallas kernels: none -> 1.3 us  [shards(): pl.pallas_call(hand_over, out_shape=(jax.ShapeDtypeStruct((1, 1, SLOTS),...]
    slice x1 -> x0, local copies, waits for them, and re-layouts: 1.28 us -> none  [shards(): return (result[0], result[1:])]
    squeeze x1 -> x0, local copies, waits for them, and re-layouts: 1.26 us -> none  [shards(): return (result[0], result[1:])]
where the time goes in v3:
time: 85.6 us; the launch traced here: 85.5 us
  Pallas kernels  84.2 us (98%)
  between operations  1.29 us (2%)
    pallas_call x1, Pallas kernels, shards(): pl.pallas_call(kernel, out_shape=jax.ShapeDtypeStruct((4, 1, 1, SLOTS), f...  82.9 us

profile of v3, /device:TPU:1, one launch (start us, length us, event | category | flops | bytes accessed | tf_op | source)
XLA Modules:
  0.0 85.5 jit_solution(5970787933454341366)
XLA Ops:
  1.3 82.9 %shard_map.140.result = f32[4,1,1,512]{3,2,1,0:T(1,128)} custom-call(f32[1,1,512]{2,1,0:T(1,128)} %charges_any.1, s32[3,1,1,512]{3,2,1,0:T(1,128)} %cells_any.1, f32[3,1,1,512]{3,2,1,0:T(1,128)} %fractions_any.1, s32[1,1]{1,0:T(1,128)S(6)} %copy.15.filled, bf16[512,384]{1,0:T(8,128)(2,1)} %constant.18.clone.line_hi_any, ...), custom_call_target="tpu_custom_call" | custom-call | tf_op jit(solution)/shard_map/pallas_call | solution.py:729
  84.2 1.3 %shard_map.141 = (f32[1,1,512]{2,1,0:T(1,128)}, f32[3,1,1,512]{3,2,1,0:T(1,128)}) custom-call(f32[4,1,1,512]{3,2,1,0:T(1,128)} %shard_map.140.result), custom_call_target="tpu_custom_call" | custom-call | tf_op jit(solution)/shard_map/pallas_call | solution.py:792

commit v4 on v3

--- a/solution.py
+++ b/solution.py
@@ -440,6 +440,7 @@
 
     core_me = lax.rem(px, 2)
     low_me = lax.div(px, 2)
+    z_me = 4 * lax.div(py, 16) + low_me
     x_me = lax.rem(lax.div(py, 4), 4)
     y_me = lax.rem(py, 4)
 
@@ -472,39 +473,47 @@
             device_id_type=MESH,
         ).start()
 
-    def send_even(group, step):
-        line = lax.rem(order + step, 128)
-        low, to_y = lax.div(line, N_PY), lax.rem(line, N_PY)
-        send_line(group, line, 2 * low + main_core(low, to_y), to_y)
-
-    def send_odd(group, step):
-        pair = lax.rem(lax.div(order, 2) + step, 64)
-        low = lax.div(pair, 16)
-        to_y = 2 * lax.rem(pair, 16)
-        to_y = to_y + lax.rem(low + lax.div(to_y, 4), 2)
-        send_line(group, 128 + pair, 2 * low + 1 - main_core(low, to_y), to_y)
+    def move_along_z(phase):
+        far = lax.div(phase + 1, 2)
+        return 4 + (2 * lax.rem(phase, 2) - 1) * -far
+
+    def send_even(group, low, high, x, move_y):
+        to_y = 16 * high + 4 * x + lax.rem(y_me + move_y, 4)
+        send_line(group, N_PY * low + to_y, 2 * low + main_core(low, to_y), to_y)
+
+    def send_odd(group, low, high, x, move_pair):
+        pair = lax.rem(lax.div(y_me, 2) + move_pair, 2)
+        to_y = 16 * high + 4 * x + 2 * pair + lax.rem(low + x, 2)
+        line = 128 + 16 * low + 8 * high + 2 * x + pair
+        send_line(group, line, 2 * low + 1 - main_core(low, to_y), to_y)
 
     def send_group(group):
+        def send_column(move_z, move_x, skip=0):
+            z = lax.rem(z_me + move_z, 8)
+            low, high = lax.rem(z, 4), lax.div(z, 4)
+            x = lax.rem(x_me + move_x, 4)
+            for k in range(skip, 4):
+                send_even(group, low, high, x, k)
+            for k in range(min(skip, 1), 2):
+                send_odd(group, low, high, x, k)
+
+        def send_far(step, carry):
+            send_column(move_along_z(lax.div(step, 4)), lax.rem(step, 4))
+            slope_block(28 * group + step)
+            return carry
+
+        def send_near(step, carry):
+            send_column(0, step)
+            return carry
+
+        lax.fori_loop(0, 28, send_far, 0)
+        lax.fori_loop(1, 4, send_near, 0)
+        send_column(0, 0, skip=1)
+        high = lax.div(py, 16)
         pl.when(active)(lambda: keep_line(group))
-        pl.when(other_me == 1)(lambda: send_even(group, 0))
-        pl.when(jnp.logical_not(matching))(lambda: send_odd(group, 0))
+        pl.when(other_me == 1)(lambda: send_even(group, low_me, high, x_me, 0))
+        pl.when(jnp.logical_not(matching))(lambda: send_odd(group, low_me, high, x_me, 0))
         pl.when(jnp.logical_not(last))(lambda: send_line(group, LINES - 1, 1, 1))
-        send_even(group, 1)
-
-        def send_evens(step, carry):
-            for k in range(7):
-                send_even(group, 2 + 7 * step + k)
-            slope_block(27 * group + step)
-            return carry
-
-        def send_odds(step, carry):
-            for k in range(7):
-                send_odd(group, 1 + 7 * step + k)
-            slope_block(27 * group + 18 + step)
-            return carry
-
-        lax.fori_loop(0, 18, send_evens, 0)
-        lax.fori_loop(0, 9, send_odds, 0)
 
     send_group(0)
     grid[second[0] * HALF : CELLS] = spread(0, True)
@@ -575,15 +584,23 @@
                 second_hi[:, j * LANES : (j + 1) * LANES] = high
                 second_lo[:, j * LANES : (j + 1) * LANES] = low
 
-        def send_row(group, other):
+        def send_row(group, to_x, to_y):
+            other = N_PY * to_x + to_y
             pltpu.make_async_remote_copy(
                 part(returning, group, other),
                 part(returned, group, line_me),
                 back_send.at[group],
                 back_recv.at[group],
-                device_id=(lax.div(other, N_PY), lax.rem(other, N_PY)),
+                device_id=(to_x, to_y),
                 device_id_type=MESH,
             ).start()
+
+        def send_rows(group, move_core, move_z, move_x, skip=0):
+            z = lax.rem(z_me + move_z, 8)
+            to_x = 2 * lax.rem(z, 4) + lax.rem(core_me + move_core, 2)
+            base = 16 * lax.div(z, 4) + 4 * lax.rem(x_me + move_x, 4)
+            for k in range(skip, 4):
+                send_row(group, to_x, base + lax.rem(y_me + k, 4))
 
         for group in range(2):
             for begin, end in pairs(group):
@@ -599,13 +616,19 @@
                     crossed = swap(mixed[COUNT:, at : at + LANES])
                     returning[j] = jnp.where(left, upper, -upper) - crossed
 
-            def send_back(step, carry, group=group):
-                for k in range(5):
-                    send_row(group, lax.rem(me + 1 + 5 * step + k, COUNT))
+            def send_far(step, carry, group=group):
+                phase = lax.div(step, 8)
+                send_rows(group, lax.rem(lax.div(step, 4), 2), move_along_z(phase), lax.rem(step, 4))
                 return carry
 
+            def send_near(step, carry, group=group):
+                send_rows(group, lax.div(step, 4), 0, lax.rem(step, 4))
+                return carry
+
+            lax.fori_loop(0, 56, send_far, 0)
+            lax.fori_loop(1, 8, send_near, 0)
+            send_rows(group, 0, 0, 0, skip=1)
             pltpu.make_async_copy(part(returning, group, me), part(returned, group, line_me), back_recv.at[group]).start()
-            lax.fori_loop(0, (COUNT - 1) // 5, send_back, 0)
 
     def restore(group):
         begin, end = GROUPS[group][:2]

time: 85.6 us -> 84.4 us (0.986)
  Pallas kernels: 84.2 us -> 83 us
    pallas_call x1, Pallas kernels: 82.9 us -> 81.7 us  [shards(): pl.pallas_call(kernel, out_shape=jax.ShapeDtypeStruct((4, 1, 1, SLOTS), f...]
where the time goes in v4:
time: 84.4 us; the launch traced here: 84.2 us
  Pallas kernels  83 us (98%)
  between operations  1.29 us (2%)
    pallas_call x1, Pallas kernels, shards(): pl.pallas_call(kernel, out_shape=jax.ShapeDtypeStruct((4, 1, 1, SLOTS), f...  81.7 us

profile of v4, /device:TPU:1, one launch (start us, length us, event | category | flops | bytes accessed | tf_op | source)
XLA Modules:
  0.0 84.2 jit_solution(9579370187348586544)
XLA Ops:
  1.3 81.7 %shard_map.140.result = f32[4,1,1,512]{3,2,1,0:T(1,128)} custom-call(f32[1,1,512]{2,1,0:T(1,128)} %charges_any.1, s32[3,1,1,512]{3,2,1,0:T(1,128)} %cells_any.1, f32[3,1,1,512]{3,2,1,0:T(1,128)} %fractions_any.1, s32[1,1]{1,0:T(1,128)S(6)} %copy.15.filled, bf16[512,384]{1,0:T(8,128)(2,1)} %constant.18.clone.line_hi_any, ...), custom_call_target="tpu_custom_call" | custom-call | tf_op jit(solution)/shard_map/pallas_call | solution.py:752
  82.9 1.3 %shard_map.141 = (f32[1,1,512]{2,1,0:T(1,128)}, f32[3,1,1,512]{3,2,1,0:T(1,128)}) custom-call(f32[4,1,1,512]{3,2,1,0:T(1,128)} %shard_map.140.result), custom_call_target="tpu_custom_call" | custom-call | tf_op jit(solution)/shard_map/pallas_call | solution.py:815

commit v5 on v4

--- a/solution.py
+++ b/solution.py
@@ -196,7 +196,7 @@
     charges_any,
     cells_any,
     fractions_any,
-    filled,
+    filled_any,
     line_hi_any,
     line_lo_any,
     brick_hi_any,
@@ -210,6 +210,7 @@
     charges,
     cells,
     fractions,
+    filled,
     line_green,
     line_hi,
     line_lo,
@@ -267,7 +268,7 @@
     arguments = [
         pltpu.make_async_copy(source, target, table_sems.at[9 + number])
         for number, (source, target) in enumerate(
-            [(charges_any, charges), (cells_any, cells), (fractions_any, fractions)]
+            [(charges_any, charges), (cells_any, cells), (fractions_any, fractions), (filled_any, filled)]
         )
     ]
     for copy in arguments:
@@ -473,9 +474,9 @@
             device_id_type=MESH,
         ).start()
 
-    def move_along_z(phase):
+    def farthest(middle, phase):
         far = lax.div(phase + 1, 2)
-        return 4 + (2 * lax.rem(phase, 2) - 1) * -far
+        return middle + (2 * lax.rem(phase, 2) - 1) * -far
 
     def send_even(group, low, high, x, move_y):
         to_y = 16 * high + 4 * x + lax.rem(y_me + move_y, 4)
@@ -492,13 +493,13 @@
             z = lax.rem(z_me + move_z, 8)
             low, high = lax.rem(z, 4), lax.div(z, 4)
             x = lax.rem(x_me + move_x, 4)
-            for k in range(skip, 4):
+            for k in [far for far in (2, 1, 3, 0) if far >= skip]:
                 send_even(group, low, high, x, k)
             for k in range(min(skip, 1), 2):
                 send_odd(group, low, high, x, k)
 
         def send_far(step, carry):
-            send_column(move_along_z(lax.div(step, 4)), lax.rem(step, 4))
+            send_column(farthest(4, lax.div(step, 4)), farthest(2, lax.rem(step, 4)))
             slope_block(28 * group + step)
             return carry
 
@@ -599,7 +600,7 @@
             z = lax.rem(z_me + move_z, 8)
             to_x = 2 * lax.rem(z, 4) + lax.rem(core_me + move_core, 2)
             base = 16 * lax.div(z, 4) + 4 * lax.rem(x_me + move_x, 4)
-            for k in range(skip, 4):
+            for k in [far for far in (2, 1, 3, 0) if far >= skip]:
                 send_row(group, to_x, base + lax.rem(y_me + k, 4))
 
         for group in range(2):
@@ -618,7 +619,7 @@
 
             def send_far(step, carry, group=group):
                 phase = lax.div(step, 8)
-                send_rows(group, lax.rem(lax.div(step, 4), 2), move_along_z(phase), lax.rem(step, 4))
+                send_rows(group, lax.rem(lax.div(step, 4), 2), farthest(4, phase), farthest(2, lax.rem(step, 4)))
                 return carry
 
             def send_near(step, carry, group=group):
@@ -752,12 +753,13 @@
     result = pl.pallas_call(
         kernel,
         out_shape=jax.ShapeDtypeStruct((4, 1, 1, SLOTS), f32),
-        in_specs=[distant] * 3 + [whole] + [distant] * 9,
+        in_specs=[distant] * 13,
         out_specs=whole,
         scratch_shapes=[
             vmem((1, 1, SLOTS), f32),
             vmem((3, 1, 1, SLOTS), jnp.int32),
             vmem((3, 1, 1, SLOTS), f32),
+            vmem((1, 1), jnp.int32),
             vmem((ROWS, 2 * LANES), f32),
             vmem((2 * PADDED, GRID), bf16),
             vmem((2 * PADDED, GRID), bf16),
@@ -797,7 +799,7 @@
             vmem((CELLS, 2 * SLOTS), f32),
             vmem((4, 8, SLOTS), f32),
             vmem((4, 8, SLOTS), f32),
-            pltpu.SemaphoreType.DMA((12,)),
+            pltpu.SemaphoreType.DMA((13,)),
             pltpu.SemaphoreType.DMA((4,)),
             pltpu.SemaphoreType.DMA((4,)),
             pltpu.SemaphoreType.DMA((2,)),

time: 84.4 us -> 84.1 us (level)
  no operation moved by 1% of the time
where the time goes in v5:
time: 84.1 us; the launch traced here: 84 us
  Pallas kernels  82.7 us (98%)
  between operations  1.29 us (2%)
    pallas_call x1, Pallas kernels, shards(): pl.pallas_call(kernel, out_shape=jax.ShapeDtypeStruct((4, 1, 1, SLOTS), f...  81.4 us

profile of v5, /device:TPU:1, one launch (start us, length us, event | category | flops | bytes accessed | tf_op | source)
XLA Modules:
  0.0 84.0 jit_solution(1028836034136289525)
XLA Ops:
  1.3 81.4 %shard_map.140.result = f32[4,1,1,512]{3,2,1,0:T(1,128)} custom-call(f32[1,1,512]{2,1,0:T(1,128)} %charges_any.1, s32[3,1,1,512]{3,2,1,0:T(1,128)} %cells_any.1, f32[3,1,1,512]{3,2,1,0:T(1,128)} %fractions_any.1, s32[1,1]{1,0:T(1,128)S(6)} %copy.15.filled_any, bf16[512,384]{1,0:T(8,128)(2,1)} %constant.18.clone.line_hi_any, ...), custom_call_target="tpu_custom_call" | custom-call | tf_op jit(solution)/shard_map/pallas_call | solution.py:753
  82.7 1.3 %shard_map.141 = (f32[1,1,512]{2,1,0:T(1,128)}, f32[3,1,1,512]{3,2,1,0:T(1,128)}) custom-call(f32[4,1,1,512]{3,2,1,0:T(1,128)} %shard_map.140.result), custom_call_target="tpu_custom_call" | custom-call | tf_op jit(solution)/shard_map/pallas_call | solution.py:817
